TPU v7x, 128 devices: a whole 4x4x4 slice. The times are simulated.
128 devices in a mesh: strike: 8 (over y, core), normal: 16 (over z, x).
Axes of the slice: x: 4, y: 4, z: 4, core: 2. Of those that a mesh axis runs over, the one named last changes fastest.
Arguments:
- displacement: float32 [3, 64, 256, 512], P(None, 'strike', 'normal'), may hold values from -4 to 4
- body_force: float32 [3, 64, 256, 512], P(None, 'strike', 'normal'), may hold values from -6 to 6
- stiffness: float32 [64, 256, 512], P('strike', 'normal'), may hold values from 0.5 to 4
- aperture_base: float32 [64, 512], P('strike', 'normal'), may hold values from 0.5 to 1.5
- contact_open: int32 [64, 512], P('strike', 'normal'), may hold values 0 or 1
- pressure_init: float32 [64, 512], P('strike', 'normal'), may hold values from -4 to 4
- injection: float32 [64, 512], P('strike', 'normal'), may hold values from -6 to 6
Outputs:
- displacement_out: float32 [3, 64, 256, 512], P(None, 'strike', 'normal')
- pressure_out: float32 [64, 512], P('strike', 'normal')
All inputs are finite; a program needn't handle non-finite values. No bound on the sum of `contact_open` on one device may be relied on, other than what follows from the above.
Results may differ from a plain program's by a relative error of at most 0.00002.
Values sent between devices are 32-bit elements; how exact they have to be, the bound alone decides.
A program may use at most 64 MiB of HBM per device.

v0:
```python
import jax
import jax.numpy as jnp
from jax import lax
from jax.sharding import PartitionSpec as P

ITERS = 2
SW_E = 4
SW_L = 6


WEIGHT_TABLE = ((2.0, 1.0, 1.0), (1.0, 2.0, 1.0), (1.0, 1.0, 2.0))
OMEGA = 0.8
TRACTION = 0.5
STORAGE = 0.5


def padded(cells, sides, width):
    for axis, dim in sides:
        count = lax.axis_size(axis)
        ends = count - 1
        head = lax.slice_in_dim(cells, 0, width, axis=dim)
        tail = lax.slice_in_dim(cells, cells.shape[dim] - width, cells.shape[dim], axis=dim)
        cells = jnp.concatenate(
            [
                lax.ppermute(tail, axis, [(i, (i + 1) % count) for i in range(ends)]),
                cells,
                lax.ppermute(head, axis, [((i + 1) % count, i) for i in range(ends)]),
            ],
            axis=dim,
        )
    return cells


def sweep_block(extended, stiff, force):
    table = jnp.array(WEIGHT_TABLE, jnp.float32)
    weight_x = table[:, 0].reshape(3, 1, 1, 1)
    weight_y = table[:, 1].reshape(3, 1, 1, 1)
    weight_z = table[:, 2].reshape(3, 1, 1, 1)
    center = extended[:, 1:-1, 1:-1, :]
    lap_x = 2.0 * center - extended[:, 2:, 1:-1, :] - extended[:, :-2, 1:-1, :]
    lap_y = 2.0 * center - extended[:, 1:-1, 2:, :] - extended[:, 1:-1, :-2, :]
    z_padded = jnp.pad(center, ((0, 0), (0, 0), (0, 0), (1, 1)))
    lap_z = 2.0 * center - z_padded[..., 2:] - z_padded[..., :-2]
    applied = stiff[None] * (weight_x * lap_x + weight_y * lap_y + weight_z * lap_z)
    return center + OMEGA * (force - applied) / (8.0 * stiff[None])


def elastic(u, stiffness, force):
    for sweep_count in range(SW_E):
        extended = padded(u, (("strike", 1), ("normal", 2)), 1)
        u = sweep_block(extended, stiffness, force)
    return u


def relax(p_ext, k_ext, base):
    conduct = k_ext[1:-1, 1:-1]
    rows = base.shape[0]
    cols = base.shape[1]
    numer = jnp.zeros_like(base)
    denom = jnp.zeros_like(base)
    for sx, sy in ((2, 1), (0, 1), (1, 2), (1, 0)):
        k_near = k_ext[sx : sx + rows, sy : sy + cols]
        p_near = p_ext[sx : sx + rows, sy : sy + cols]
        face = 0.5 * (conduct + k_near)
        numer = numer + face * p_near
        denom = denom + face
    return (base + numer) / (STORAGE + denom)


def lubricate(pressure, conduct, base):
    k_ext = padded(conduct, (("strike", 0), ("normal", 1)), 1)
    for sweep_count in range(SW_L):
        p_ext = padded(pressure, (("strike", 0), ("normal", 1)), 1)
        pressure = relax(p_ext, k_ext, base)
    return pressure


def body(
    displacement, body_force, stiffness, aperture_base, contact_open, pressure_init, injection
):
    u = displacement
    pressure = pressure_init
    normal_index = lax.axis_index("normal")
    half = lax.axis_size("normal") // 2
    for step in range(ITERS):
        whole_pressure = lax.all_gather(pressure, "normal", axis=1, tiled=True)
        add_above = jnp.where(normal_index == half, TRACTION * whole_pressure, 0.0)
        add_below = jnp.where(normal_index == half - 1, -(TRACTION * whole_pressure), 0.0)
        force = body_force.at[1, :, 0, :].add(add_above)
        force = force.at[1, :, -1, :].add(add_below)
        u = elastic(u, stiffness, force)
        top_row = u[1, :, 0, :]
        bottom_row = u[1, :, -1, :]
        contrib = jnp.where(normal_index == half, top_row, 0.0) - jnp.where(
            normal_index == half - 1, bottom_row, 0.0
        )
        opening = lax.psum_scatter(contrib, "normal", scatter_dimension=1, tiled=True)
        width = aperture_base + jax.nn.softplus(opening)
        conduct = contact_open.astype(jnp.float32) * (width * width * width) / 12.0
        base = STORAGE * pressure - opening + injection
        pressure = lubricate(pressure, conduct, base)
    return (u, pressure)


def solution(mesh):
    in_specs = (
        P(None, "strike", "normal", None),
        P(None, "strike", "normal", None),
        P("strike", "normal", None),
        P("strike", "normal"),
        P("strike", "normal"),
        P("strike", "normal"),
        P("strike", "normal"),
    )
    out_specs = (P(None, "strike", "normal", None), P("strike", "normal"))
    return jax.shard_map(body, mesh=mesh, in_specs=in_specs, out_specs=out_specs, check_vma=False)
```

profile of v0, /device:TPU:40, one launch (start us, length us, event | category | flops | bytes accessed | tf_op | source)
XLA Modules:
  0.0 570.8 jit_solution(14649533620142427899)
XLA Ops:
  14.1 24.2 %all-gather = f32[16,32,8]{1,2,0:T(8,128)S(1)} all-gather(f32[1,32,8]{1,2,0:T(8,128)S(1)} %bitcast.45), channel_id=1, replica_groups=mesh['strike'=8,'normal'=16] {'normal'}, dimensions={0}, use_global_device_ids=true | all-gather | bytes 17408 | tf_op jit(solution)/shard_map/all_gather | solution.py:86
  40.8 4.6 collective-permute-start.2
  47.7 6.3 %collective-permute-done.3 = f32[3,10,1,512]{3,1,2,0:T(8,128)S(1)} collective-permute-done((f32[3,10,1,512]{3,1,2,0:T(8,128)S(1)}, f32[3,10,1,512]{3,1,2,0:T(8,128)S(1)}, u32[]{:S(2)}, u32[]{:S(2)}) %collective-permute-start.3) | collective-permute-done | bytes 61472 | tf_op jit(solution)/shard_map/ppermute | solution.py:25
  65.0 3.9 collective-permute-start.7
  69.6 4.0 collective-permute-done.7
  84.6 3.9 collective-permute-start.11
  89.2 4.0 collective-permute-done.11
  105.8 3.9 collective-permute-start.15
  110.8 4.0 collective-permute-done.15
  118.8 67.6 %reduce-scatter.7.cloned.1.call-done = f32[32,8]{1,0:T(8,128)} async-done(((f32[512,8]{1,0:T(8,128)}), f32[32,8]{1,0:T(8,128)}) %reduce-scatter.7.cloned.1.call-update) | async-done | bytes 1040
  194.1 5.5 collective-permute-start.20
  201.6 5.7 collective-permute-done.22
  216.2 3.9 collective-permute-start.27
  232.7 3.9 collective-permute-start.31
  249.3 3.9 collective-permute-start.35
  266.6 3.9 collective-permute-start.39
  283.7 3.9 collective-permute-start.43
  291.4 21.4 %all-gather.1 = f32[16,32,8]{1,2,0:T(8,128)S(1)} all-gather(f32[1,32,8]{1,2,0:T(8,128)S(1)} %bitcast.44), channel_id=1, replica_groups=mesh['strike'=8,'normal'=16] {'normal'}, dimensions={0}, use_global_device_ids=true | all-gather | bytes 17408 | tf_op jit(solution)/shard_map/all_gather | solution.py:86
  313.1 4.6 collective-permute-start.46
  319.9 6.4 %collective-permute-done.47 = f32[3,10,1,512]{3,1,2,0:T(8,128)S(1)} collective-permute-done((f32[3,10,1,512]{3,1,2,0:T(8,128)S(1)}, f32[3,10,1,512]{3,1,2,0:T(8,128)S(1)}, u32[]{:S(2)}, u32[]{:S(2)}) %collective-permute-start.47) | collective-permute-done | bytes 61472 | tf_op jit(solution)/shard_map/ppermute | solution.py:25
  337.3 3.9 collective-permute-start.51
  341.9 4.0 collective-permute-done.51
  356.9 3.9 collective-permute-start.55
  361.5 4.0 collective-permute-done.55
  378.1 3.9 collective-permute-start.59
  383.4 4.0 collective-permute-done.59
  391.3 68.4 %reduce-scatter.9.cloned.1.call-done = f32[32,8]{1,0:T(8,128)} async-done(((f32[512,8]{1,0:T(8,128)}), f32[32,8]{1,0:T(8,128)}) %reduce-scatter.9.cloned.1.call-update) | async-done | bytes 1040
  467.4 5.5 collective-permute-start.64
  474.9 5.7 collective-permute-done.66
  489.5 3.9 collective-permute-start.71
  506.1 3.9 collective-permute-start.75
  522.6 3.9 collective-permute-start.79
  (281 shorter events, 250.1 us)
Async XLA Ops:
  7.2 179.2 %reduce-scatter.7.cloned.1.call-start = ((), (), s32[]{:S(2)}) async-start(), calls=%async_computation.2 | async-start | bytes 278528
  8.4 32.4 %collective-permute-start = (f32[3,1,16,512]{3,1,2,0:T(1,128)S(1)}, f32[3,1,16,512]{3,1,2,0:T(1,128)S(1)}, u32[]{:S(2)}, u32[]{:S(2)}) collective-permute-start(f32[3,1,16,512]{3,1,2,0:T(1,128)S(1)} %copy.55), channel_id=1, source_target_pairs={{16,0},{32,16},{48,32},{64,48},{80,64},{96,80},{112,96},{17,1},{33... | collective-permute-start | bytes 294920 | tf_op jit(solution)/shard_map/ppermute | solution.py:27
  11.0 29.7 %collective-permute-start.1 = (f32[3,1,16,512]{3,1,2,0:T(1,128)}, f32[3,1,16,512]{3,1,2,0:T(1,128)S(1)}, u32[]{:S(2)}, u32[]{:S(2)}) collective-permute-start(f32[3,1,16,512]{3,1,2,0:T(1,128)} %copy.57), channel_id=1, source_target_pairs={{0,16},{16,32},{32,48},{48,64},{64,80},{80,96},{96,112},{1,17},{17... | collective-permute-start | bytes 294920 | tf_op jit(solution)/shard_map/ppermute | solution.py:25
  45.4 8.6 %collective-permute-start.3 = (f32[3,10,1,512]{3,1,2,0:T(8,128)S(1)}, f32[3,10,1,512]{3,1,2,0:T(8,128)S(1)}, u32[]{:S(2)}, u32[]{:S(2)}) collective-permute-start(f32[3,10,1,512]{3,1,2,0:T(8,128)S(1)} %get-tuple-element.79), channel_id=1, source_target_pairs={{0,1},{1,2},{2,3},{3,4},{4,5},{5,6},{6,7},{7,8},{8,9},{9,10},{10,1... | collective-permute-start | bytes 184328 | tf_op jit(solution)/shard_map/ppermute | solution.py:25
  65.0 8.6 %collective-permute-start.7 = (f32[3,10,1,512]{3,1,2,0:T(8,128)S(1)}, f32[3,10,1,512]{3,1,2,0:T(8,128)S(1)}, u32[]{:S(2)}, u32[]{:S(2)}) collective-permute-start(f32[3,10,1,512]{3,1,2,0:T(8,128)S(1)} %get-tuple-element.77), channel_id=1, source_target_pairs={{0,1},{1,2},{2,3},{3,4},{4,5},{5,6},{6,7},{7,8},{8,9},{9,10},{10,1... | collective-permute-start | bytes 184328 | tf_op jit(solution)/shard_map/ppermute | solution.py:25
  84.6 8.6 %collective-permute-start.11 = (f32[3,10,1,512]{3,1,2,0:T(8,128)S(1)}, f32[3,10,1,512]{3,1,2,0:T(8,128)S(1)}, u32[]{:S(2)}, u32[]{:S(2)}) collective-permute-start(f32[3,10,1,512]{3,1,2,0:T(8,128)S(1)} %get-tuple-element.75), channel_id=1, source_target_pairs={{0,1},{1,2},{2,3},{3,4},{4,5},{5,6},{6,7},{7,8},{8,9},{9,10},{10,1... | collective-permute-start | bytes 184328 | tf_op jit(solution)/shard_map/ppermute | solution.py:25
  94.4 9.4 %collective-permute-start.12 = (f32[3,1,16,512]{3,1,2,0:T(1,128)S(1)}, f32[3,1,16,512]{3,1,2,0:T(1,128)S(1)}, u32[]{:S(2)}, u32[]{:S(2)}) collective-permute-start(f32[3,1,16,512]{3,1,2,0:T(1,128)S(1)} %get-tuple-element.89), channel_id=1, source_target_pairs={{16,0},{32,16},{48,32},{64,48},{80,64},{96,80},{112,96},{17,1},{33... | collective-permute-start | bytes 294920 | tf_op jit(solution)/shard_map/ppermute | solution.py:27
  98.7 11.0 %collective-permute-start.17 = (f32[1,32]{1,0:T(1,128)S(1)}, f32[1,32]{1,0:T(1,128)S(1)}, u32[]{:S(2)}, u32[]{:S(2)}) collective-permute-start(f32[1,32]{1,0:T(1,128)S(1)} %get-tuple-element.155), channel_id=1, source_target_pairs={{16,0},{32,16},{48,32},{64,48},{80,64},{96,80},{112,96},{17,1},{33... | collective-permute-start | bytes 392 | tf_op jit(solution)/shard_map/ppermute | solution.py:27
  101.9 7.9 %collective-permute-start.19 = (f32[1,32]{1,0:T(1,128)S(1)}, f32[1,32]{1,0:T(1,128)S(1)}, u32[]{:S(2)}, u32[]{:S(2)}) collective-permute-start(f32[1,32]{1,0:T(1,128)S(1)} %get-tuple-element.154), channel_id=1, source_target_pairs={{0,16},{16,32},{32,48},{48,64},{64,80},{80,96},{96,112},{1,17},{17... | collective-permute-start | bytes 392 | tf_op jit(solution)/shard_map/ppermute | solution.py:25
  105.8 9.0 %collective-permute-start.15 = (f32[3,10,1,512]{3,1,2,0:T(8,128)S(1)}, f32[3,10,1,512]{3,1,2,0:T(8,128)S(1)}, u32[]{:S(2)}, u32[]{:S(2)}) collective-permute-start(f32[3,10,1,512]{3,1,2,0:T(8,128)S(1)} %get-tuple-element.73), channel_id=1, source_target_pairs={{0,1},{1,2},{2,3},{3,4},{4,5},{5,6},{6,7},{7,8},{8,9},{9,10},{10,1... | collective-permute-start | bytes 184328 | tf_op jit(solution)/shard_map/ppermute | solution.py:25
  116.7 343.0 %reduce-scatter.9.cloned.1.call-start = ((), (), s32[]{:S(2)}) async-start(), calls=%async_computation.3 | async-start | bytes 278528
  116.8 84.7 %collective-permute-start.21 = (f32[10,1]{1,0:T(8,128)S(1)}, f32[10,1]{1,0:T(8,128)S(1)}, u32[]{:S(2)}, u32[]{:S(2)}) collective-permute-start(f32[10,1]{1,0:T(8,128)S(1)} %get-tuple-element.126), channel_id=1, source_target_pairs={{1,0},{2,1},{3,2},{4,3},{5,4},{6,5},{7,6},{8,7},{9,8},{10,9},{11,1... | collective-permute-start | bytes 128 | tf_op jit(solution)/shard_map/ppermute | solution.py:27
  191.6 10.0 %collective-permute-start.23 = (f32[10,1]{1,0:T(8,128)S(1)}, f32[10,1]{1,0:T(8,128)S(1)}, u32[]{:S(2)}, u32[]{:S(2)}) collective-permute-start(f32[10,1]{1,0:T(8,128)S(1)} %get-tuple-element.127), channel_id=1, source_target_pairs={{0,1},{1,2},{2,3},{3,4},{4,5},{5,6},{6,7},{7,8},{8,9},{9,10},{10,1... | collective-permute-start | bytes 128 | tf_op jit(solution)/shard_map/ppermute | solution.py:25
  199.7 7.7 %collective-permute-start.22 = (f32[10,1]{1,0:T(8,128)S(1)}, f32[10,1]{1,0:T(8,128)S(1)}, u32[]{:S(2)}, u32[]{:S(2)}) collective-permute-start(f32[10,1]{1,0:T(8,128)S(1)} %get-tuple-element.124), channel_id=1, source_target_pairs={{0,1},{1,2},{2,3},{3,4},{4,5},{5,6},{6,7},{7,8},{8,9},{9,10},{10,1... | collective-permute-start | bytes 128 | tf_op jit(solution)/shard_map/ppermute | solution.py:25
  216.2 7.7 %collective-permute-start.27 = (f32[10,1]{1,0:T(8,128)S(1)}, f32[10,1]{1,0:T(8,128)S(1)}, u32[]{:S(2)}, u32[]{:S(2)}) collective-permute-start(f32[10,1]{1,0:T(8,128)S(1)} %get-tuple-element.123), channel_id=1, source_target_pairs={{0,1},{1,2},{2,3},{3,4},{4,5},{5,6},{6,7},{7,8},{8,9},{9,10},{10,1... | collective-permute-start | bytes 128 | tf_op jit(solution)/shard_map/ppermute | solution.py:25
  232.7 7.7 %collective-permute-start.31 = (f32[10,1]{1,0:T(8,128)S(1)}, f32[10,1]{1,0:T(8,128)S(1)}, u32[]{:S(2)}, u32[]{:S(2)}) collective-permute-start(f32[10,1]{1,0:T(8,128)S(1)} %get-tuple-element.121), channel_id=1, source_target_pairs={{0,1},{1,2},{2,3},{3,4},{4,5},{5,6},{6,7},{7,8},{8,9},{9,10},{10,1... | collective-permute-start | bytes 128 | tf_op jit(solution)/shard_map/ppermute | solution.py:25
  249.3 7.7 %collective-permute-start.35 = (f32[10,1]{1,0:T(8,128)S(1)}, f32[10,1]{1,0:T(8,128)S(1)}, u32[]{:S(2)}, u32[]{:S(2)}) collective-permute-start(f32[10,1]{1,0:T(8,128)S(1)} %get-tuple-element.119), channel_id=1, source_target_pairs={{0,1},{1,2},{2,3},{3,4},{4,5},{5,6},{6,7},{7,8},{8,9},{9,10},{10,1... | collective-permute-start | bytes 128 | tf_op jit(solution)/shard_map/ppermute | solution.py:25
  261.4 51.7 %collective-permute-start.44 = (f32[3,1,16,512]{3,1,2,0:T(1,128)S(1)}, f32[3,1,16,512]{3,1,2,0:T(1,128)S(1)}, u32[]{:S(2)}, u32[]{:S(2)}) collective-permute-start(f32[3,1,16,512]{3,1,2,0:T(1,128)S(1)} %get-tuple-element.87), channel_id=1, source_target_pairs={{16,0},{32,16},{48,32},{64,48},{80,64},{96,80},{112,96},{17,1},{33... | collective-permute-start | bytes 294920 | tf_op jit(solution)/shard_map/ppermute | solution.py:27
  266.6 7.7 %collective-permute-start.39 = (f32[10,1]{1,0:T(8,128)S(1)}, f32[10,1]{1,0:T(8,128)S(1)}, u32[]{:S(2)}, u32[]{:S(2)}) collective-permute-start(f32[10,1]{1,0:T(8,128)S(1)} %get-tuple-element.117), channel_id=1, source_target_pairs={{0,1},{1,2},{2,3},{3,4},{4,5},{5,6},{6,7},{7,8},{8,9},{9,10},{10,1... | collective-permute-start | bytes 128 | tf_op jit(solution)/shard_map/ppermute | solution.py:25
  278.6 34.4 %collective-permute-start.45 = (f32[3,1,16,512]{3,1,2,0:T(1,128)S(1)}, f32[3,1,16,512]{3,1,2,0:T(1,128)S(1)}, u32[]{:S(2)}, u32[]{:S(2)}) collective-permute-start(f32[3,1,16,512]{3,1,2,0:T(1,128)S(1)} %get-tuple-element.86), channel_id=1, source_target_pairs={{0,16},{16,32},{32,48},{48,64},{64,80},{80,96},{96,112},{1,17},{17... | collective-permute-start | bytes 294920 | tf_op jit(solution)/shard_map/ppermute | solution.py:25
  283.7 7.7 %collective-permute-start.43 = (f32[10,1]{1,0:T(8,128)S(1)}, f32[10,1]{1,0:T(8,128)S(1)}, u32[]{:S(2)}, u32[]{:S(2)}) collective-permute-start(f32[10,1]{1,0:T(8,128)S(1)} %get-tuple-element.115), channel_id=1, source_target_pairs={{0,1},{1,2},{2,3},{3,4},{4,5},{5,6},{6,7},{7,8},{8,9},{9,10},{10,1... | collective-permute-start | bytes 128 | tf_op jit(solution)/shard_map/ppermute | solution.py:25
  317.7 8.6 %collective-permute-start.47 = (f32[3,10,1,512]{3,1,2,0:T(8,128)S(1)}, f32[3,10,1,512]{3,1,2,0:T(8,128)S(1)}, u32[]{:S(2)}, u32[]{:S(2)}) collective-permute-start(f32[3,10,1,512]{3,1,2,0:T(8,128)S(1)} %get-tuple-element.71), channel_id=1, source_target_pairs={{0,1},{1,2},{2,3},{3,4},{4,5},{5,6},{6,7},{7,8},{8,9},{9,10},{10,1... | collective-permute-start | bytes 184328 | tf_op jit(solution)/shard_map/ppermute | solution.py:25
  337.3 8.6 %collective-permute-start.51 = (f32[3,10,1,512]{3,1,2,0:T(8,128)S(1)}, f32[3,10,1,512]{3,1,2,0:T(8,128)S(1)}, u32[]{:S(2)}, u32[]{:S(2)}) collective-permute-start(f32[3,10,1,512]{3,1,2,0:T(8,128)S(1)} %get-tuple-element.69), channel_id=1, source_target_pairs={{0,1},{1,2},{2,3},{3,4},{4,5},{5,6},{6,7},{7,8},{8,9},{9,10},{10,1... | collective-permute-start | bytes 184328 | tf_op jit(solution)/shard_map/ppermute | solution.py:25
  356.9 8.6 %collective-permute-start.55 = (f32[3,10,1,512]{3,1,2,0:T(8,128)S(1)}, f32[3,10,1,512]{3,1,2,0:T(8,128)S(1)}, u32[]{:S(2)}, u32[]{:S(2)}) collective-permute-start(f32[3,10,1,512]{3,1,2,0:T(8,128)S(1)} %get-tuple-element.67), channel_id=1, source_target_pairs={{0,1},{1,2},{2,3},{3,4},{4,5},{5,6},{6,7},{7,8},{8,9},{9,10},{10,1... | collective-permute-start | bytes 184328 | tf_op jit(solution)/shard_map/ppermute | solution.py:25
  366.7 9.4 %collective-permute-start.56 = (f32[3,1,16,512]{3,1,2,0:T(1,128)S(1)}, f32[3,1,16,512]{3,1,2,0:T(1,128)S(1)}, u32[]{:S(2)}, u32[]{:S(2)}) collective-permute-start(f32[3,1,16,512]{3,1,2,0:T(1,128)S(1)} %get-tuple-element.81), channel_id=1, source_target_pairs={{16,0},{32,16},{48,32},{64,48},{80,64},{96,80},{112,96},{17,1},{33... | collective-permute-start | bytes 294920 | tf_op jit(solution)/shard_map/ppermute | solution.py:27
  371.0 11.0 %collective-permute-start.61 = (f32[1,32]{1,0:T(1,128)S(1)}, f32[1,32]{1,0:T(1,128)S(1)}, u32[]{:S(2)}, u32[]{:S(2)}) collective-permute-start(f32[1,32]{1,0:T(1,128)S(1)} %get-tuple-element.141), channel_id=1, source_target_pairs={{16,0},{32,16},{48,32},{64,48},{80,64},{96,80},{112,96},{17,1},{33... | collective-permute-start | bytes 392 | tf_op jit(solution)/shard_map/ppermute | solution.py:27
  374.2 7.9 %collective-permute-start.63 = (f32[1,32]{1,0:T(1,128)S(1)}, f32[1,32]{1,0:T(1,128)S(1)}, u32[]{:S(2)}, u32[]{:S(2)}) collective-permute-start(f32[1,32]{1,0:T(1,128)S(1)} %get-tuple-element.140), channel_id=1, source_target_pairs={{0,16},{16,32},{32,48},{48,64},{64,80},{80,96},{96,112},{1,17},{17... | collective-permute-start | bytes 392 | tf_op jit(solution)/shard_map/ppermute | solution.py:25
  378.1 9.4 %collective-permute-start.59 = (f32[3,10,1,512]{3,1,2,0:T(8,128)S(1)}, f32[3,10,1,512]{3,1,2,0:T(8,128)S(1)}, u32[]{:S(2)}, u32[]{:S(2)}) collective-permute-start(f32[3,10,1,512]{3,1,2,0:T(8,128)S(1)} %get-tuple-element.65), channel_id=1, source_target_pairs={{0,1},{1,2},{2,3},{3,4},{4,5},{5,6},{6,7},{7,8},{8,9},{9,10},{10,1... | collective-permute-start | bytes 184328 | tf_op jit(solution)/shard_map/ppermute | solution.py:25
  389.4 85.5 %collective-permute-start.65 = (f32[10,1]{1,0:T(8,128)S(1)}, f32[10,1]{1,0:T(8,128)S(1)}, u32[]{:S(2)}, u32[]{:S(2)}) collective-permute-start(f32[10,1]{1,0:T(8,128)S(1)} %get-tuple-element.112), channel_id=1, source_target_pairs={{1,0},{2,1},{3,2},{4,3},{5,4},{6,5},{7,6},{8,7},{9,8},{10,9},{11,1... | collective-permute-start | bytes 128 | tf_op jit(solution)/shard_map/ppermute | solution.py:27
  464.9 10.0 %collective-permute-start.67 = (f32[10,1]{1,0:T(8,128)S(1)}, f32[10,1]{1,0:T(8,128)S(1)}, u32[]{:S(2)}, u32[]{:S(2)}) collective-permute-start(f32[10,1]{1,0:T(8,128)S(1)} %get-tuple-element.113), channel_id=1, source_target_pairs={{0,1},{1,2},{2,3},{3,4},{4,5},{5,6},{6,7},{7,8},{8,9},{9,10},{10,1... | collective-permute-start | bytes 128 | tf_op jit(solution)/shard_map/ppermute | solution.py:25
  489.5 7.7 %collective-permute-start.71 = (f32[10,1]{1,0:T(8,128)S(1)}, f32[10,1]{1,0:T(8,128)S(1)}, u32[]{:S(2)}, u32[]{:S(2)}) collective-permute-start(f32[10,1]{1,0:T(8,128)S(1)} %get-tuple-element.109), channel_id=1, source_target_pairs={{0,1},{1,2},{2,3},{3,4},{4,5},{5,6},{6,7},{7,8},{8,9},{9,10},{10,1... | collective-permute-start | bytes 128 | tf_op jit(solution)/shard_map/ppermute | solution.py:25
  539.1 7.7 %collective-permute-start.83 = (f32[10,1]{1,0:T(8,128)S(1)}, f32[10,1]{1,0:T(8,128)S(1)}, u32[]{:S(2)}, u32[]{:S(2)}) collective-permute-start(f32[10,1]{1,0:T(8,128)S(1)} %get-tuple-element.103), channel_id=1, source_target_pairs={{0,1},{1,2},{2,3},{3,4},{4,5},{5,6},{6,7},{7,8},{8,9},{9,10},{10,1... | collective-permute-start | bytes 128 | tf_op jit(solution)/shard_map/ppermute | solution.py:25
  (68 other events, 406.5 us)
Sparse Core Ops, SparseCore 0:
  116.8 69.4 reduce-scatter.6
  389.5 70.2 reduce-scatter.8
where the time goes:
time: 574 us; the launch traced here: 571 us
  waiting for transfers between devices  259 us (45%)
  starting transfers between devices  228 us (40%)
  blocking collectives  45.6 us (8%)
  between operations  15.6 us (3%)
  local copies, waits for them, and re-layouts  12 us (2%)
  other arithmetic  10.2 us (2%)
    unnamed x4, waiting for transfers between devices  136 us
    ppermute x44, starting transfers between devices, padded(): lax.ppermute(tail, axis, [(i, (i + 1) % count) for i in range(ends)])  128 us
    ppermute x44, waiting for transfers between devices, padded(): lax.ppermute(tail, axis, [(i, (i + 1) % count) for i in range(ends)])  118 us
    ppermute x44, starting transfers between devices, padded(): lax.ppermute(head, axis, [((i + 1) % count, i) for i in range(ends)])  101 us
    all_gather x2, blocking collectives, body(): whole_pressure = lax.all_gather(pressure, 'normal', axis=1, tiled=True)  45.6 us
  transfers between devices with their start and end apart: 90, of which 43 were waited for; matrix products, arithmetic and copies ran while one was open for 1% of the time, Pallas kernels for 0%

commit v1 on v0

v1 whole, which is shorter than its diff:
```python
import jax
import jax.numpy as jnp
from jax import lax
from jax.experimental import pallas as pl
from jax.experimental.pallas import tpu as pltpu
from jax.sharding import PartitionSpec as P

MESH = pl.DeviceIdType.MESH
F32 = jnp.float32
NS, NN = 8, 16
HS, HN, DIP = 8, 16, 512
SW = 4
SW_L = 6
O = 5
LANES = 128
NJ = DIP // LANES
WAYS = (-1, 1)


def lane_pair(x, lane):
    left, right = [], []
    rl = [pltpu.roll(v, 1, 1) for v in x]
    rr = [pltpu.roll(v, LANES - 1, 1) for v in x]
    for j in range(NJ):
        left.append(jnp.where(lane == 0, rl[j - 1] if j else 0.0, rl[j]))
        right.append(jnp.where(lane == LANES - 1, rr[j + 1] if j < NJ - 1 else 0.0, rr[j]))
    return left, right


def cols(j):
    return slice(j * LANES, (j + 1) * LANES)


def lane_sums(x, first, last):
    width = x.shape[1]
    return (jnp.where(first, 0.0, pltpu.roll(x, 1, 1)), jnp.where(last, 0.0, pltpu.roll(x, width - 1, 1)))


def rows_sums(x):
    count = x.shape[0]
    return pltpu.roll(x, 1, 0), pltpu.roll(x, count - 1, 0)


def kernel(
    u_in, f_in, st_in, ap_in, ct_in, p_in, inj_in,
    u_out, p_out,
    xb, gb, st, outb, rs, rn, sn, rc, sc, pk, gath, plw, qw, r4, r8, row, tt, tx, corr, p1w, p2t, e4s, e4r,
    in_sem, out_sem, s_snd, s_rcv, n_snd, n_rcv, c_snd, c_rcv, g_snd, g_rcv,
    q_snd, q_rcv, w_snd, w_rcv, r4_snd, r4_rcv, r8_snd, r8_rcv, e4_snd, e4_rcv,
):
    s = lax.axis_index("strike")
    n = lax.axis_index("normal")
    is_a = n == NN // 2 - 1
    is_b = n == NN // 2
    is_i = jnp.logical_or(is_a, is_b)
    side = jnp.where(n >= NN // 2, 1, 0)
    has_s = {-1: s > 0, 1: s < NS - 1}
    has_n = {-1: n > 0, 1: n < NN - 1}
    lane = lax.broadcasted_iota(jnp.int32, (8, LANES), 1)
    sub = lax.broadcasted_iota(jnp.int32, (8, LANES), 0)
    sub5 = lax.broadcasted_iota(jnp.int32, (8, DIP), 0)

    order = (1, 0, 2)
    loads = {"st": pltpu.make_async_copy(st_in, st, in_sem.at[6])}
    for c in range(3):
        loads["u", c] = pltpu.make_async_copy(
            u_in.at[c], xb.at[0, c, 0, pl.ds(O, HS), pl.ds(0, HN)], in_sem.at[c]
        )
        loads["f", c] = pltpu.make_async_copy(f_in.at[c], gb.at[c, pl.ds(O, HS)], in_sem.at[3 + c])
    loads["st"].start()
    for c in order:
        loads["f", c].start()
        loads["u", c].start()

    barrier = pltpu.get_barrier_semaphore()
    count = jnp.int32(0)

    def greet(cond, target):
        @pl.when(cond)
        def _():
            pl.semaphore_signal(barrier, inc=1, device_id=target, device_id_type=MESH)

        return jnp.where(cond, 1, 0)

    for a in WAYS:
        count += greet(has_s[a], (s + a, n))
        count += greet(has_n[a], (s, n + a))
        for b in WAYS:
            count += greet(jnp.logical_and(has_s[a], has_n[b]), (s + a, n + b))
    for mid in (NN // 2 - 1, NN // 2):
        count += greet(n != mid, (s, mid))
    for other in range(NN):
        count += greet(jnp.logical_and(is_i, n != other), (s, other))

    def in_range(j):
        return jnp.logical_and(s + (j - 2) >= 0, s + (j - 2) <= NS - 1)

    for j in range(5):
        ok = jnp.logical_and(is_i, in_range(j))
        if j != 2:
            count += greet(ok, (s + (j - 2), n))
        count += greet(ok, (s + (j - 2), NN - 1 - n))

    zrow = jnp.zeros((24, DIP), F32)

    def clear(i, carry):
        for c in range(3):
            for rd in range(2):
                lo = i
                for pp in range(2):
                    xb[rd, c, pp, jnp.where(lo < 4, lo + 1 - pp, lo + 9 + pp)] = zrow
            gb[c, jnp.where(i < 4, i + 1, i + 9)] = jnp.zeros((HN, DIP), F32)
        for c in range(3):
            for rd in range(2):
                xb[rd, c, 0, O + i, pl.ds(16, 8), :] = jnp.zeros((8, DIP), F32)
        return carry

    lax.fori_loop(0, 8, clear, 0)

    for a, w in ((-1, 0), (1, 1)):
        @pl.when(jnp.logical_not(has_s[a]))
        def _():
            rs[:, :, w] = jnp.zeros((2, 3, 4, HN, DIP), F32)

        @pl.when(jnp.logical_not(has_n[a]))
        def _():
            rn[:, :, w] = jnp.zeros((2, 3, 4, 8, DIP), F32)

        for b, v in ((-1, 0), (1, 1)):
            @pl.when(jnp.logical_not(jnp.logical_and(has_s[a], has_n[b])))
            def _():
                rc[:, :, w, v] = jnp.zeros((2, 3, 8, DIP), F32)

    @pl.when(is_i)
    def _():
        tx[...] = jnp.zeros_like(tx)
        for j in range(5):
            @pl.when(jnp.logical_not(in_range(j)))
            def _():
                plw[j] = jnp.zeros((4, 8, DIP), F32)
                qw[:, j] = jnp.zeros((2, 8, DIP), F32)
                r4[:, j] = jnp.zeros((2, 8, DIP), F32)
                if 1 <= j <= 3:
                    r8[:, j - 1] = jnp.zeros((2, 8, DIP), F32)

    pk[...] = jnp.concatenate(
        [p_in[...], ap_in[...], ct_in[...].astype(F32), inj_in[...]], axis=1
    )

    pl.semaphore_wait(barrier, count)

    gathers = []
    for k, mid in enumerate((NN // 2 - 1, NN // 2)):
        gathers.append(
            (
                n != mid,
                pltpu.make_async_remote_copy(
                    src_ref=pk, dst_ref=gath.at[n], send_sem=g_snd.at[k], recv_sem=g_rcv,
                    device_id=(s, mid), device_id_type=MESH,
                ),
            )
        )
    for cond, copy in gathers:
        pl.when(cond)(copy.start)

    loads["st"].wait()

    def recip(i, carry):
        st[i] = 0.1 / st[i]
        return carry

    lax.fori_loop(0, HS, recip, 0)

    @pl.when(is_a)
    def _():
        for i in range(HS):
            qw[0, 2, i : i + 1, :] = 0.5 * st[i, HN - 1 : HN, :]

    @pl.when(is_b)
    def _():
        for i in range(HS):
            qw[0, 2, i : i + 1, :] = 0.5 * st[i, 0:1, :]

    def row_copies(buf, snd, rcv, first, last, src):
        out = []
        for rel in range(2):
            for j in range(first, last):
                if rel == 0 and j == 2:
                    continue
                target_n = n if rel == 0 else NN - 1 - n
                snd_copy = pltpu.make_async_remote_copy(
                    src_ref=src, dst_ref=buf.at[rel, 4 - j - first], send_sem=snd.at[rel, j - first],
                    recv_sem=rcv.at[rel, 4 - j - first], device_id=(s + (j - 2), target_n), device_id_type=MESH,
                )
                rcv_copy = pltpu.make_async_remote_copy(
                    src_ref=src, dst_ref=buf.at[rel, j - first], send_sem=snd.at[rel, j - first],
                    recv_sem=rcv.at[rel, j - first], device_id=(s + (j - 2), target_n), device_id_type=MESH,
                )
                out.append((in_range(j), snd_copy, rcv_copy))
        return out

    q_copies = row_copies(qw, q_snd, q_rcv, 0, 5, qw.at[0, 2])
    r4_copies = row_copies(r4, r4_snd, r4_rcv, 0, 5, r4.at[0, 2])
    r8_copies = row_copies(r8, r8_snd, r8_rcv, 1, 4, r8.at[0, 1])
    w_copies = []
    for j in (0, 1, 3, 4):
        w_copies.append(
            (
                in_range(j),
                pltpu.make_async_remote_copy(
                    src_ref=plw.at[2], dst_ref=plw.at[4 - j], send_sem=w_snd.at[j], recv_sem=w_rcv.at[4 - j],
                    device_id=(s + (j - 2), n), device_id_type=MESH,
                ),
                pltpu.make_async_remote_copy(
                    src_ref=plw.at[2], dst_ref=plw.at[j], send_sem=w_snd.at[j], recv_sem=w_rcv.at[j],
                    device_id=(s + (j - 2), n), device_id_type=MESH,
                ),
            )
        )

    def send_rows(copies):
        for cond, snd, _ in copies:
            pl.when(cond)(snd.start)

    def get_rows(copies):
        for cond, _, rcv in copies:
            pl.when(cond)(rcv.wait_recv)

    def end_rows(copies):
        for cond, snd, _ in copies:
            pl.when(cond)(snd.wait_send)

    @pl.when(is_i)
    def _():
        send_rows(q_copies)

    keep_hi = jnp.logical_or(has_n[1], sub >= 4)
    keep_lo = jnp.logical_or(has_n[-1], sub < 4)
    keep = jnp.logical_and(keep_hi, keep_lo)

    def sweeps(rd, c):
        ax, ay, az = [0.2 if c == k else 0.1 for k in range(3)]

        def sweep(k, carry):
            src = lax.rem(k - 1, 2)
            dst = lax.rem(k, 2)
            lo = jnp.where(has_s[-1], O - k, O)
            hi = jnp.where(has_s[1], O + HS + k, O + HS)

            def one(i, inner):
                x = [[xb[rd, c, src, i, t * 8 : t * 8 + 8, cols(j)] for j in range(NJ)] for t in range(3)]
                up = [[pltpu.roll(v, 1, 0) for v in r] for r in x]
                dn = [[pltpu.roll(v, 7, 0) for v in r] for r in x]
                for t in range(3):
                    left, right = lane_pair(x[t], lane)
                    for j in range(NJ):
                        xm = xb[rd, c, src, i - 1, t * 8 : t * 8 + 8, cols(j)]
                        xp = xb[rd, c, src, i + 1, t * 8 : t * 8 + 8, cols(j)]
                        sy = jnp.where(sub == 0, up[(t + 2) % 3][j], up[t][j]) + jnp.where(
                            sub == 7, dn[(t + 1) % 3][j], dn[t][j]
                        )
                        sx = xm + xp
                        sz = left[j] + right[j]
                        if c == 0:
                            val = 0.2 * (x[t][j] + sx) + 0.1 * (sy + sz)
                        elif c == 1:
                            val = 0.2 * (x[t][j] + sy) + 0.1 * (sx + sz)
                        else:
                            val = 0.2 * (x[t][j] + sz) + 0.1 * (sx + sy)
                        if t < 2:
                            val = val + gb[c, i, t * 8 : t * 8 + 8, cols(j)]
                        else:
                            val = jnp.where(keep, val, 0.0)
                        xb[rd, c, dst, i, t * 8 : t * 8 + 8, cols(j)] = val
                return inner

            lax.fori_loop(lo, hi, one, 0)
            return carry

        lax.fori_loop(1, SW + 1, sweep, 0)

    def messages(rd, c):
        out = []
        for a, w in ((-1, 0), (1, 1)):
            first = 1 if a < 0 else O + HS
            out.append(
                (
                    has_s[a],
                    pltpu.make_async_remote_copy(
                        src_ref=xb.at[rd, c, 0, pl.ds(first, 4), pl.ds(0, HN)], dst_ref=rs.at[rd, c, 1 - w],
                        send_sem=s_snd.at[rd, c, w], recv_sem=s_rcv.at[rd, c, 1 - w],
                        device_id=(s + a, n), device_id_type=MESH,
                    ),
                    pltpu.make_async_remote_copy(
                        src_ref=rs.at[rd, c, w], dst_ref=rs.at[rd, c, w],
                        send_sem=s_snd.at[rd, c, w], recv_sem=s_rcv.at[rd, c, w],
                        device_id=(s + a, n), device_id_type=MESH,
                    ),
                )
            )
        for b, v in ((-1, 0), (1, 1)):
            out.append(
                (
                    has_n[b],
                    pltpu.make_async_remote_copy(
                        src_ref=sn.at[rd, c, v], dst_ref=rn.at[rd, c, 1 - v],
                        send_sem=n_snd.at[rd, c, v], recv_sem=n_rcv.at[rd, c, 1 - v],
                        device_id=(s, n + b), device_id_type=MESH,
                    ),
                    pltpu.make_async_remote_copy(
                        src_ref=sn.at[rd, c, v], dst_ref=rn.at[rd, c, v],
                        send_sem=n_snd.at[rd, c, v], recv_sem=n_rcv.at[rd, c, v],
                        device_id=(s, n + b), device_id_type=MESH,
                    ),
                )
            )
        for a, w in ((-1, 0), (1, 1)):
            for b, v in ((-1, 0), (1, 1)):
                out.append(
                    (
                        jnp.logical_and(has_s[a], has_n[b]),
                        pltpu.make_async_remote_copy(
                            src_ref=sc.at[rd, c, w, v], dst_ref=rc.at[rd, c, 1 - w, 1 - v],
                            send_sem=c_snd.at[rd, c, w, v], recv_sem=c_rcv.at[rd, c, 1 - w, 1 - v],
                            device_id=(s + a, n + b), device_id_type=MESH,
                        ),
                        pltpu.make_async_remote_copy(
                            src_ref=sc.at[rd, c, w, v], dst_ref=rc.at[rd, c, w, v],
                            send_sem=c_snd.at[rd, c, w, v], recv_sem=c_rcv.at[rd, c, w, v],
                            device_id=(s + a, n + b), device_id_type=MESH,
                        ),
                    )
                )
        return out

    msgs = {(rd, c): messages(rd, c) for rd in range(2) for c in range(3)}
    r4sub = sub5 < 4

    def ghost(rd, c, i):
        return xb[rd, c, 0, i, 16:24, :]

    def send(rd, c):
        group = msgs[rd, c]
        for cond, snd, _ in group[:2]:
            pl.when(cond)(snd.start)
        for w in range(2):
            g = [ghost(rd, c, O - d if w == 0 else O + HS - 1 + d) for d in (1, 2, 3)]
            sc[rd, c, w, 1] = jnp.where(
                r4sub, g[0], jnp.where(sub5 < 6, pltpu.roll(g[1], 4, 0), pltpu.roll(g[2], 6, 0))
            )
            sc[rd, c, w, 0] = jnp.where(
                r4sub, jnp.where(sub5 >= 2, pltpu.roll(g[1], 4, 0), pltpu.roll(g[2], 2, 0)), g[0]
            )
        for cond, snd, _ in group[4:]:
            pl.when(cond)(snd.start)
        for t in range(4):
            first, second = ghost(rd, c, O + t), ghost(rd, c, O + t + 4)
            sn[rd, c, 1, t] = jnp.where(r4sub, first, pltpu.roll(second, 4, 0))
            sn[rd, c, 0, t] = jnp.where(r4sub, pltpu.roll(first, 4, 0), second)
        for cond, snd, _ in group[2:4]:
            pl.when(cond)(snd.start)

    def merge(rd, c, store):
        for cond, _, rcv in msgs[rd, c]:
            pl.when(cond)(rcv.wait_recv)
        for i in range(HS):
            t = i % 4
            low = xb[rd, c, 0, O + i, 0:8, :]
            high = xb[rd, c, 0, O + i, 8:16, :]
            way = 0 if i < 4 else 1
            low = low + rs[rd, c, way, t, 0:8, :]
            high = high + rs[rd, c, way, t, 8:16, :]
            from_lo, from_hi = rn[rd, c, 0, t], rn[rd, c, 1, t]
            if i < 4:
                from_hi = pltpu.roll(from_hi, 4, 0)
            else:
                from_lo = pltpu.roll(from_lo, 4, 0)
            low = low + jnp.where(r4sub, from_lo, 0.0)
            high = high + jnp.where(r4sub, 0.0, from_hi)
            d = i + 1 if i < 4 else HS - i
            if d <= 3:
                corner_lo, corner_hi = rc[rd, c, way, 0], rc[rd, c, way, 1]
                if d == 1:
                    low = low + jnp.where(r4sub, corner_lo, 0.0)
                    high = high + jnp.where(r4sub, 0.0, corner_hi)
                elif d == 2:
                    low = low + jnp.where(sub5 < 2, pltpu.roll(corner_lo, 4, 0), 0.0)
                    high = high + jnp.where(sub5 >= 6, pltpu.roll(corner_hi, 4, 0), 0.0)
                else:
                    low = low + jnp.where(sub5 < 2, pltpu.roll(corner_lo, 2, 0), 0.0)
                    high = high + jnp.where(sub5 >= 6, pltpu.roll(corner_hi, 6, 0), 0.0)
            store(i, low, high)

    def traction(p_of, q_of):
        for r in range(-3, HS + 3):
            p_row = p_of(r)
            own = p_row * q_of(0, r)
            far = p_row * q_of(1, r)
            below = jnp.where(is_b, far, own)
            above = jnp.where(is_b, own, far)
            tt[r + 3] = jnp.where(sub5 == 3, -below, jnp.where(sub5 == 4, above, 0.0))

        def tile_sweep(src, dst, lo, hi, shift):
            def one(i, carry):
                x = [src[i, :, cols(j)] for j in range(NJ)]
                left, right = lane_pair(x, lane)
                for j in range(NJ):
                    sy = pltpu.roll(x[j], 1, 0) + pltpu.roll(x[j], 7, 0)
                    sx = src[i - 1, :, cols(j)] + src[i + 1, :, cols(j)]
                    dst[i - shift, :, cols(j)] = (
                        0.2 * (x[j] + sy) + 0.1 * (sx + left[j] + right[j]) + tt[i, :, cols(j)]
                    )
                return carry

            lax.fori_loop(jnp.where(has_s[-1], lo, 3), jnp.where(has_s[1], hi, 11), one, 0)

        tile_sweep(tt, tx.at[0], 1, 13, 0)
        tile_sweep(tx.at[0], tx.at[1], 2, 12, 0)
        tile_sweep(tx.at[1], corr, 3, 11, 3)

    def win_row(ref, r):
        j, i = divmod(r + 16, 8)
        return ref(j)[i : i + 1, :]

    def lubricate(opening, p, ap, ct, inj, first_row):
        rows = opening.shape[0]
        lanes = lax.broadcasted_iota(jnp.int32, (rows, DIP), 1)
        first, last = lanes == 0, lanes == DIP - 1
        strike = lax.broadcasted_iota(jnp.int32, (rows, DIP), 0) + (s * HS + first_row)
        valid = jnp.logical_and(strike >= 0, strike < NS * HS)
        soft = jnp.maximum(opening, 0.0) + jnp.log1p(jnp.exp(-jnp.abs(opening)))
        width = ap + soft
        k = ct * (width * width * width) / 12.0
        base = 0.5 * p - opening + inj
        k_up, k_dn = rows_sums(k)
        k_l, k_r = lane_sums(k, first, last)
        f_up, f_dn, f_l, f_r = [0.5 * (k + v) for v in (k_up, k_dn, k_l, k_r)]
        rden = jnp.where(valid, 1.0 / (0.5 + (f_up + f_dn + f_l + f_r)), 0.0)
        base = base * rden
        f_up, f_dn = f_up * rden, f_dn * rden
        f_l = jnp.where(first, 0.0, f_l * rden)
        f_r = jnp.where(last, 0.0, f_r * rden)
        for _ in range(SW_L):
            p_up, p_dn = rows_sums(p)
            p = base + f_up * p_up + f_dn * p_dn + f_l * pltpu.roll(p, 1, 1) + f_r * pltpu.roll(p, DIP - 1, 1)
        return p

    sign = jnp.where(is_b, 1.0, -1.0)

    for c in order:
        loads["f", c].wait()

        def scale(i, carry, c=c):
            gb[c, O + i] = gb[c, O + i] * st[i]
            return carry

        lax.fori_loop(0, HS, scale, 0)
        loads["u", c].wait()
        sweeps(0, c)
        send(0, c)

    @pl.when(is_i)
    def _():
        gath[n] = pk[...]
        pltpu.make_async_copy(gath.at[pl.ds(0, NN - 1)], gath.at[pl.ds(0, NN - 1)], g_rcv).wait()
        for big in range(NJ):
            tiles = [gath[big * 4 + m] for m in range(4)]
            for kind in range(4):
                val = None
                for m in range(4):
                    shift = (m - kind) % 4 * 32
                    piece = pltpu.roll(tiles[m], shift, 1) if shift else tiles[m]
                    val = piece if val is None else jnp.where(lane >= 32 * m, piece, val)
                plw[2, kind, :, cols(big)] = val
        send_rows(w_copies)
        get_rows(q_copies)
        get_rows(w_copies)
        traction(
            lambda r: win_row(lambda j: plw[j, 0], r), lambda rel, r: win_row(lambda j: qw[rel, j], r)
        )

    def to_second(c):
        def store(i, low, high):
            xb[1, c, 0, O + i, 0:8, :] = low
            xb[1, c, 0, O + i, 8:16, :] = high

        return store

    def to_out(c):
        def store(i, low, high):
            outb[c, i, 0:8, :] = low
            outb[c, i, 8:16, :] = high

        return store

    def own_tile(get, put):
        @pl.when(is_a)
        def _():
            for i in range(HS):
                put(i, 8, get(i, 8) + jnp.where(r4sub, 0.0, pltpu.roll(corr[i], 4, 0)))

        @pl.when(is_b)
        def _():
            for i in range(HS):
                put(i, 0, get(i, 0) + jnp.where(r4sub, pltpu.roll(corr[i], 4, 0), 0.0))

    def put_rows(get, put):
        @pl.when(is_a)
        def _():
            for i in range(HS):
                put(i, get(i, HN - 1))

        @pl.when(is_b)
        def _():
            for i in range(HS):
                put(i, get(i, 0))

    def put_second(i, r, v):
        xb[1, 1, 0, O + i, r : r + 8, :] = v

    def put_out(i, r, v):
        outb[1, i, r : r + 8, :] = v

    def put_r4(i, v):
        r4[0, 2, i : i + 1, :] = v

    def put_r8(i, v):
        r8[0, 1, i : i + 1, :] = v

    for c in order:
        merge(0, c, to_second(c))
        if c == 1:
            own_tile(lambda i, r: xb[1, 1, 0, O + i, r : r + 8, :], put_second)
            put_rows(lambda i, r: xb[1, 1, 0, O + i, r : r + 1, :], put_r4)
            pl.when(is_i)(lambda: send_rows(r4_copies))
        sweeps(1, c)
        send(1, c)

    def flat(x):
        return x.reshape(x.shape[0] * 8, DIP)

    @pl.when(is_i)
    def _():
        get_rows(r4_copies)
        opening = sign * (flat(r4[0]) - flat(r4[1]))
        p1 = lubricate(opening, *[flat(plw[:, kind]) for kind in range(4)], -16)
        p1w[...] = p1.reshape(5, 8, DIP)
        traction(
            lambda r: win_row(lambda j: p1w[j], r), lambda rel, r: win_row(lambda j: qw[rel, j], r)
        )

    copies_out = [pltpu.make_async_copy(outb.at[c], u_out.at[c], out_sem.at[c]) for c in range(3)]
    for c in order:
        merge(1, c, to_out(c))
        if c == 1:
            put_rows(lambda i, r: outb[1, i, r : r + 1, :], put_r8)
            pl.when(is_i)(lambda: send_rows(r8_copies))
            own_tile(lambda i, r: outb[1, i, r : r + 8, :], put_out)
        copies_out[c].start()

    e4_copies = []
    for i in range(NN // 2):
        e4_copies.append(
            (
                jnp.logical_and(is_i, n != side * 8 + i),
                pltpu.make_async_remote_copy(
                    src_ref=e4s.at[i], dst_ref=e4r, send_sem=e4_snd.at[i], recv_sem=e4_rcv,
                    device_id=(s, side * 8 + i), device_id_type=MESH,
                ),
            )
        )

    @pl.when(is_i)
    def _():
        lanes = lax.broadcasted_iota(jnp.int32, (40, DIP), 1)
        first, last = lanes == 0, lanes == DIP - 1
        strike = lax.broadcasted_iota(jnp.int32, (40, DIP), 0) + (s * HS - 16)
        valid = jnp.logical_and(strike >= 0, strike < NS * HS)

        def across(x):
            up, dn = rows_sums(x)
            left, right = lane_sums(x, first, last)
            return 0.1 * ((up + dn) + (left + right))

        force = flat(p1w[...]) * (flat(qw[0]) + flat(qw[1]))
        d0 = jnp.where(valid, across(force) + force, 0.0)
        d1 = 0.2 * force
        e0 = jnp.where(valid, 0.2 * d1 + across(d0) + force, 0.0)
        e1 = jnp.where(valid, 0.2 * d1 + across(d1) + 0.2 * d0, 0.0)
        extra = (0.2 * e1 + across(e0) + force)[8:32]
        get_rows(r8_copies)
        opening = sign * (flat(r8[0]) - flat(r8[1])) + extra
        p2 = lubricate(
            opening, flat(p1w[1:4]), flat(plw[1:4, 1]), flat(plw[1:4, 2]), flat(plw[1:4, 3]), -8
        )
        for j in range(NJ):
            p2t[j] = p2[8:16, cols(j)]
        for i in range(NN // 2):
            shift = -(i % 4) * 32 % LANES
            tile = p2t[side * 2 + i // 4]
            e4s[i] = pltpu.roll(tile, shift, 1) if shift else tile
        for cond, copy in e4_copies:
            pl.when(cond)(copy.start)
        e4r[...] = e4s[jnp.where(is_b, 0, 7)]

    @pl.when(jnp.logical_not(is_i))
    def _():
        pltpu.make_async_remote_copy(
            src_ref=e4s.at[0], dst_ref=e4r, send_sem=e4_snd.at[0], recv_sem=e4_rcv,
            device_id=(s, NN - 1 - n), device_id_type=MESH,
        ).wait_recv()

    p_out[...] = e4r[:, 0:32]

    for copy in copies_out:
        copy.wait()
    for group in msgs.values():
        for cond, snd, _ in group:
            pl.when(cond)(snd.wait_send)
    for cond, copy in gathers:
        pl.when(cond)(copy.wait_send)
    for cond, copy in e4_copies:
        pl.when(cond)(copy.wait_send)

    @pl.when(is_i)
    def _():
        for copies in (q_copies, w_copies, r4_copies, r8_copies):
            end_rows(copies)


def body(displacement, body_force, stiffness, aperture_base, contact_open, pressure_init, injection):
    vm = pl.BlockSpec(memory_space=pltpu.VMEM)
    hbm = pl.BlockSpec(memory_space=pl.ANY)
    dma = pltpu.SemaphoreType.DMA

    def buf(*shape):
        return pltpu.VMEM(shape, F32)

    scratch = [
        buf(2, 3, 2, 18, 24, DIP),
        buf(3, 18, HN, DIP),
        buf(HS, HN, DIP),
        buf(3, HS, HN, DIP),
        buf(2, 3, 2, 4, HN, DIP),
        buf(2, 3, 2, 4, 8, DIP),
        buf(2, 3, 2, 4, 8, DIP),
        buf(2, 3, 2, 2, 8, DIP),
        buf(2, 3, 2, 2, 8, DIP),
        buf(8, LANES),
        buf(NN, 8, LANES),
        buf(5, 4, 8, DIP),
        buf(2, 5, 8, DIP),
        buf(2, 5, 8, DIP),
        buf(2, 3, 8, DIP),
        buf(8, DIP),
        buf(14, 8, DIP),
        buf(2, 14, 8, DIP),
        buf(HS, 8, DIP),
        buf(5, 8, DIP),
        buf(NJ, 8, LANES),
        buf(NN // 2, 8, LANES),
        buf(8, LANES),
        dma((7,)), dma((3,)),
        dma((2, 3, 2)), dma((2, 3, 2)), dma((2, 3, 2)), dma((2, 3, 2)),
        dma((2, 3, 2, 2)), dma((2, 3, 2, 2)),
        dma((2,)), dma,
        dma((2, 5)), dma((2, 5)), dma((5,)), dma((5,)), dma((2, 5)), dma((2, 5)), dma((2, 3)), dma((2, 3)),
        dma((NN // 2,)), dma,
    ]
    return pl.pallas_call(
        kernel,
        out_shape=(
            jax.ShapeDtypeStruct((3, HS, HN, DIP), F32),
            jax.ShapeDtypeStruct((8, 32), F32),
        ),
        in_specs=[hbm, hbm, hbm, vm, vm, vm, vm],
        out_specs=(hbm, vm),
        scratch_shapes=scratch,
        compiler_params=pltpu.CompilerParams(
            collective_id=0, has_side_effects=True, vmem_limit_bytes=48 * 2**20
        ),
        cost_estimate=pl.CostEstimate(flops=60_000_000, bytes_accessed=2_700_000, transcendentals=40_000),
    )(displacement, body_force, stiffness, aperture_base, contact_open, pressure_init, injection)


def solution(mesh):
    in_specs = (
        P(None, "strike", "normal", None),
        P(None, "strike", "normal", None),
        P("strike", "normal", None),
        P("strike", "normal"),
        P("strike", "normal"),
        P("strike", "normal"),
        P("strike", "normal"),
    )
    out_specs = (P(None, "strike", "normal", None), P("strike", "normal"))
    return jax.shard_map(body, mesh=mesh, in_specs=in_specs, out_specs=out_specs, check_vma=False)
```

time: 574 us -> 87.1 us (0.15)
  the two profiles are of different devices: /device:TPU:40 before, /device:TPU:1 now
where the time goes in v1:
time: 87.1 us; the launch traced here: 86.8 us
  Pallas kernels  78.7 us (90%)
  local copies, waits for them, and re-layouts  7.43 us (9%)
    pallas_call x1, Pallas kernels, body(): pl.pallas_call(kernel, out_shape=(jax.ShapeDtypeStruct((3, HS, HN, DIP),...  78.7 us
    unnamed x16, local copies, waits for them, and re-layouts  7.43 us

profile of v1, /device:TPU:1, one launch (start us, length us, event | category | flops | bytes accessed | tf_op | source)
XLA Modules:
  0.0 86.8 jit_solution(16484833333814314529)
XLA Ops:
  0.6 0.0 copy-start
  0.6 1.1 %copy-done = f32[3,8,16,512]{3,2,1,0:T(8,128)S(1)} copy-done((f32[3,8,16,512]{3,2,1,0:T(8,128)S(1)}, f32[3,8,16,512]{3,2,1,0:T(8,128)}, u32[]{:S(2)}) %copy-start) | copy-done | bytes 786456
  1.8 0.0 copy-start.1
  1.8 1.1 %copy-done.1 = f32[3,8,16,512]{3,2,1,0:T(8,128)S(1)} copy-done((f32[3,8,16,512]{3,2,1,0:T(8,128)S(1)}, f32[3,8,16,512]{3,2,1,0:T(8,128)}, u32[]{:S(2)}) %copy-start.1) | copy-done | bytes 786456
  2.9 0.0 copy-start.2
  2.9 0.9 %copy-done.2 = f32[8,16,512]{2,1,0:T(8,128)S(1)} copy-done((f32[8,16,512]{2,1,0:T(8,128)S(1)}, f32[8,16,512]{2,1,0:T(8,128)}, u32[]{:S(2)}) %copy-start.2) | copy-done | bytes 262168
  3.9 0.0 copy-start.3
  3.9 0.7 copy-done.3
  4.5 0.0 copy-start.4
  4.5 0.7 copy-done.4
  5.2 0.0 copy-start.5
  5.2 0.7 copy-done.5
  5.9 0.0 copy-start.6
  5.9 0.7 copy-done.6
  6.6 78.7 %shard_map.86 = (f32[3,8,16,512]{3,2,1,0:T(8,128)S(1)}, f32[8,32]{1,0:T(8,128)S(1)}) custom-call(f32[3,8,16,512]{3,2,1,0:T(8,128)S(1)} %copy-done, f32[3,8,16,512]{3,2,1,0:T(8,128)S(1)} %copy-done.1, f32[8,16,512]{2,1,0:T(8,128)S(1)} %copy-done.2, f32[8,32]{1,0:T(8,128)S(1)} %copy-done.3, s32[8,32]{1,0:T(8,128)S(1)} %copy-done.4, f32[8,32]{1,0:T(8,128)S(1)} %copy-done.5, ...), custom_call_target="tpu_custom_call" | custom-call | flops 60000000 | bytes 2700000 | tf_op jit(solution)/shard_map/pallas_call | solution.py:670
  85.3 0.9 %copy.11 = f32[3,8,16,512]{3,2,1,0:T(8,128)} copy(f32[3,8,16,512]{3,2,1,0:T(8,128)S(1)} %get-tuple-element.4) | data formatting | bytes 1572864
  86.2 0.6 copy.12
Async XLA Ops:
  0.6 1.1 %copy-start = (f32[3,8,16,512]{3,2,1,0:T(8,128)S(1)}, f32[3,8,16,512]{3,2,1,0:T(8,128)}, u32[]{:S(2)}) copy-start(f32[3,8,16,512]{3,2,1,0:T(8,128)} %u_in.1) | copy-start | bytes 2359300
  1.8 1.1 %copy-start.1 = (f32[3,8,16,512]{3,2,1,0:T(8,128)S(1)}, f32[3,8,16,512]{3,2,1,0:T(8,128)}, u32[]{:S(2)}) copy-start(f32[3,8,16,512]{3,2,1,0:T(8,128)} %f_in.1) | copy-start | bytes 2359300
  2.9 0.9 %copy-start.2 = (f32[8,16,512]{2,1,0:T(8,128)S(1)}, f32[8,16,512]{2,1,0:T(8,128)}, u32[]{:S(2)}) copy-start(f32[8,16,512]{2,1,0:T(8,128)} %st_in.1) | copy-start | bytes 786436
  3.9 0.7 copy-start.3
  4.5 0.7 copy-start.4
  5.2 0.7 copy-start.5
  5.9 0.7 copy-start.6

commit v2 on v1

--- a/solution.py
+++ b/solution.py
@@ -42,9 +42,9 @@
 
 
 def kernel(
-    u_in, f_in, st_in, ap_in, ct_in, p_in, inj_in,
+    u_in, f_in, st_in, ap_hbm, ct_hbm, p_hbm, inj_hbm,
     u_out, p_out,
-    xb, gb, st, outb, rs, rn, sn, rc, sc, pk, gath, plw, qw, r4, r8, row, tt, tx, corr, p1w, p2t, e4s, e4r,
+    xb, gb, st, outb, rs, rn, sn, rc, sc, pk, gath, plw, qw, r4, r8, small, ct_v, tt, tx, corr, p1w, p2t, e4s, e4r,
     in_sem, out_sem, s_snd, s_rcv, n_snd, n_rcv, c_snd, c_rcv, g_snd, g_rcv,
     q_snd, q_rcv, w_snd, w_rcv, r4_snd, r4_rcv, r8_snd, r8_rcv, e4_snd, e4_rcv,
 ):
@@ -67,6 +67,11 @@
             u_in.at[c], xb.at[0, c, 0, pl.ds(O, HS), pl.ds(0, HN)], in_sem.at[c]
         )
         loads["f", c] = pltpu.make_async_copy(f_in.at[c], gb.at[c, pl.ds(O, HS)], in_sem.at[3 + c])
+    for k, ref in enumerate((p_hbm, ap_hbm, inj_hbm)):
+        loads["small", k] = pltpu.make_async_copy(ref, small.at[k], in_sem.at[7 + k])
+        loads["small", k].start()
+    loads["ct"] = pltpu.make_async_copy(ct_hbm, ct_v, in_sem.at[10])
+    loads["ct"].start()
     loads["st"].start()
     for c in order:
         loads["f", c].start()
@@ -143,9 +148,10 @@
                 if 1 <= j <= 3:
                     r8[:, j - 1] = jnp.zeros((2, 8, DIP), F32)
 
-    pk[...] = jnp.concatenate(
-        [p_in[...], ap_in[...], ct_in[...].astype(F32), inj_in[...]], axis=1
-    )
+    for k in range(3):
+        loads["small", k].wait()
+    loads["ct"].wait()
+    pk[...] = jnp.concatenate([small[0], small[1], ct_v[...].astype(F32), small[2]], axis=1)
 
     pl.semaphore_wait(barrier, count)
 
@@ -239,42 +245,50 @@
     keep = jnp.logical_and(keep_hi, keep_lo)
 
     def sweeps(rd, c):
-        ax, ay, az = [0.2 if c == k else 0.1 for k in range(3)]
-
         def sweep(k, carry):
             src = lax.rem(k - 1, 2)
             dst = lax.rem(k, 2)
-            lo = jnp.where(has_s[-1], O - k, O)
-            hi = jnp.where(has_s[1], O + HS + k, O + HS)
-
-            def one(i, inner):
-                x = [[xb[rd, c, src, i, t * 8 : t * 8 + 8, cols(j)] for j in range(NJ)] for t in range(3)]
-                up = [[pltpu.roll(v, 1, 0) for v in r] for r in x]
-                dn = [[pltpu.roll(v, 7, 0) for v in r] for r in x]
-                for t in range(3):
-                    left, right = lane_pair(x[t], lane)
-                    for j in range(NJ):
-                        xm = xb[rd, c, src, i - 1, t * 8 : t * 8 + 8, cols(j)]
-                        xp = xb[rd, c, src, i + 1, t * 8 : t * 8 + 8, cols(j)]
-                        sy = jnp.where(sub == 0, up[(t + 2) % 3][j], up[t][j]) + jnp.where(
-                            sub == 7, dn[(t + 1) % 3][j], dn[t][j]
-                        )
-                        sx = xm + xp
-                        sz = left[j] + right[j]
-                        if c == 0:
-                            val = 0.2 * (x[t][j] + sx) + 0.1 * (sy + sz)
-                        elif c == 1:
-                            val = 0.2 * (x[t][j] + sy) + 0.1 * (sx + sz)
-                        else:
-                            val = 0.2 * (x[t][j] + sz) + 0.1 * (sx + sy)
-                        if t < 2:
-                            val = val + gb[c, i, t * 8 : t * 8 + 8, cols(j)]
-                        else:
-                            val = jnp.where(keep, val, 0.0)
-                        xb[rd, c, dst, i, t * 8 : t * 8 + 8, cols(j)] = val
+
+            def get(i):
+                return [[xb[rd, c, src, i, t * 8 : t * 8 + 8, cols(j)] for j in range(NJ)] for t in range(3)]
+
+            def pair(m, inner):
+                base = O - k + 2 * m
+                rows = [get(base - 1 + r) for r in range(2 + 2)]
+                vals = {}
+                for r in range(2):
+                    i = base + r
+                    xm, x, xp = rows[r : r + 3]
+                    ok = jnp.logical_and(
+                        jnp.logical_or(has_s[-1], i >= O), jnp.logical_or(has_s[1], i < O + HS)
+                    )
+                    one, two = jnp.where(ok, 0.1, 0.0), jnp.where(ok, 0.2, 0.0)
+                    up = [[pltpu.roll(v, 1, 0) for v in q] for q in x]
+                    dn = [[pltpu.roll(v, 7, 0) for v in q] for q in x]
+                    for t in range(3):
+                        left, right = lane_pair(x[t], lane)
+                        for j in range(NJ):
+                            sy = jnp.where(sub == 0, up[(t + 2) % 3][j], up[t][j]) + jnp.where(
+                                sub == 7, dn[(t + 1) % 3][j], dn[t][j]
+                            )
+                            sx = xm[t][j] + xp[t][j]
+                            sz = left[j] + right[j]
+                            if c == 0:
+                                val = two * (x[t][j] + sx) + one * (sy + sz)
+                            elif c == 1:
+                                val = two * (x[t][j] + sy) + one * (sx + sz)
+                            else:
+                                val = two * (x[t][j] + sz) + one * (sx + sy)
+                            if t < 2:
+                                val = val + gb[c, i, t * 8 : t * 8 + 8, cols(j)]
+                            else:
+                                val = jnp.where(keep, val, 0.0)
+                            vals[r, t, j] = val
+                for (r, t, j), val in vals.items():
+                    xb[rd, c, dst, base + r, t * 8 : t * 8 + 8, cols(j)] = val
                 return inner
 
-            lax.fori_loop(lo, hi, one, 0)
+            lax.fori_loop(0, HS // 2 + k, pair, 0)
             return carry
 
         lax.fori_loop(1, SW + 1, sweep, 0)
@@ -652,7 +666,8 @@
         buf(2, 5, 8, DIP),
         buf(2, 5, 8, DIP),
         buf(2, 3, 8, DIP),
-        buf(8, DIP),
+        buf(3, 8, 32),
+        pltpu.VMEM((8, 32), jnp.int32),
         buf(14, 8, DIP),
         buf(2, 14, 8, DIP),
         buf(HS, 8, DIP),
@@ -660,7 +675,7 @@
         buf(NJ, 8, LANES),
         buf(NN // 2, 8, LANES),
         buf(8, LANES),
-        dma((7,)), dma((3,)),
+        dma((11,)), dma((3,)),
         dma((2, 3, 2)), dma((2, 3, 2)), dma((2, 3, 2)), dma((2, 3, 2)),
         dma((2, 3, 2, 2)), dma((2, 3, 2, 2)),
         dma((2,)), dma,
@@ -673,11 +688,11 @@
             jax.ShapeDtypeStruct((3, HS, HN, DIP), F32),
             jax.ShapeDtypeStruct((8, 32), F32),
         ),
-        in_specs=[hbm, hbm, hbm, vm, vm, vm, vm],
+        in_specs=[hbm] * 7,
         out_specs=(hbm, vm),
         scratch_shapes=scratch,
         compiler_params=pltpu.CompilerParams(
-            collective_id=0, has_side_effects=True, vmem_limit_bytes=48 * 2**20
+            collective_id=0, has_side_effects=True, vmem_limit_bytes=60 * 2**20
         ),
         cost_estimate=pl.CostEstimate(flops=60_000_000, bytes_accessed=2_700_000, transcendentals=40_000),
     )(displacement, body_force, stiffness, aperture_base, contact_open, pressure_init, injection)

time: 87.1 us -> 52.8 us (0.61)
  Pallas kernels: 78.7 us -> 49.3 us
  local copies, waits for them, and re-layouts: 7.43 us -> 2.69 us
    pallas_call x1, Pallas kernels: 78.7 us -> 49.3 us  [body(): pl.pallas_call(kernel, out_shape=(jax.ShapeDtypeStruct((3, HS, HN, DIP),...]
    unnamed x16 -> x4, local copies, waits for them, and re-layouts: 7.43 us -> 2.69 us
where the time goes in v2:
time: 52.8 us; the launch traced here: 52.7 us
  Pallas kernels  49.3 us (93%)
  local copies, waits for them, and re-layouts  2.69 us (5%)
  between operations  0.65 us (1%)
    pallas_call x1, Pallas kernels, body(): pl.pallas_call(kernel, out_shape=(jax.ShapeDtypeStruct((3, HS, HN, DIP),...  49.3 us
    unnamed x4, local copies, waits for them, and re-layouts  2.69 us

profile of v2, /device:TPU:1, one launch (start us, length us, event | category | flops | bytes accessed | tf_op | source)
XLA Modules:
  0.0 52.7 jit_solution(10010030130304344147)
XLA Ops:
  0.6 49.3 %shard_map.86 = (f32[3,8,16,512]{3,2,1,0:T(8,128)}, f32[8,32]{1,0:T(8,128)}) custom-call(f32[3,8,16,512]{3,2,1,0:T(8,128)} %u_in.1, f32[3,8,16,512]{3,2,1,0:T(8,128)} %f_in.1, f32[8,16,512]{2,1,0:T(8,128)} %st_in.1, f32[8,32]{1,0:T(8,128)} %ap_hbm.1, s32[8,32]{1,0:T(8,128)} %ct_hbm.1, f32[8,32]{1,0:T(8,128)} %p_hbm.1, f32[8,32]{1,0:T(8,128)} %inj_hbm.1), custom_call_target="tpu_custom_call" | custom-call | flops 60000000 | bytes 2700000 | tf_op jit(solution)/shard_map/pallas_call | solution.py:685
  50.0 0.0 copy-start
  50.0 2.1 %copy.11 = f32[3,8,16,512]{3,2,1,0:T(8,128)} copy(f32[3,8,16,512]{3,2,1,0:T(8,128)} %get-tuple-element.4) | data formatting | bytes 1572864
  52.1 0.0 copy-done
  52.1 0.6 %copy.12 = f32[8,32]{1,0:T(8,128)} copy(f32[8,32]{1,0:T(8,128)S(1)} %copy-done) | data formatting | bytes 2048
Async XLA Ops:
  50.0 2.1 %copy-start = (f32[8,32]{1,0:T(8,128)S(1)}, f32[8,32]{1,0:T(8,128)}, u32[]{:S(2)}) copy-start(f32[8,32]{1,0:T(8,128)} %get-tuple-element.5) | copy-start | bytes 3076

commit v3 on v2

--- a/solution.py
+++ b/solution.py
@@ -18,12 +18,8 @@
 
 
 def lane_pair(x, lane):
-    left, right = [], []
-    rl = [pltpu.roll(v, 1, 1) for v in x]
-    rr = [pltpu.roll(v, LANES - 1, 1) for v in x]
-    for j in range(NJ):
-        left.append(jnp.where(lane == 0, rl[j - 1] if j else 0.0, rl[j]))
-        right.append(jnp.where(lane == LANES - 1, rr[j + 1] if j < NJ - 1 else 0.0, rr[j]))
+    left = [jnp.where(lane == 0, 0.0, pltpu.roll(x[-1], 1, 1))] + x[:-1]
+    right = x[1:] + [jnp.where(lane == LANES - 1, 0.0, pltpu.roll(x[0], LANES - 1, 1))]
     return left, right
 
 
@@ -31,9 +27,20 @@
     return slice(j * LANES, (j + 1) * LANES)
 
 
-def lane_sums(x, first, last):
-    width = x.shape[1]
-    return (jnp.where(first, 0.0, pltpu.roll(x, 1, 1)), jnp.where(last, 0.0, pltpu.roll(x, width - 1, 1)))
+def lane_shifts(x):
+    cut = DIP - LANES
+    left = jnp.concatenate([pltpu.roll(x[:, cut:], 1, 1), x[:, :cut]], axis=1)
+    right = jnp.concatenate([x[:, LANES:], pltpu.roll(x[:, :LANES], LANES - 1, 1)], axis=1)
+    return left, right
+
+
+def shuffle(x, matrix):
+    high = x.astype(jnp.bfloat16)
+    rest = x - high.astype(F32)
+    mid = rest.astype(jnp.bfloat16)
+    low = (rest - mid.astype(F32)).astype(jnp.bfloat16)
+    out = [jnp.dot(part, matrix, preferred_element_type=F32) for part in (high, mid, low)]
+    return out[0] + (out[1] + out[2])
 
 
 def rows_sums(x):
@@ -44,7 +51,7 @@
 def kernel(
     u_in, f_in, st_in, ap_hbm, ct_hbm, p_hbm, inj_hbm,
     u_out, p_out,
-    xb, gb, st, outb, rs, rn, sn, rc, sc, pk, gath, plw, qw, r4, r8, small, ct_v, tt, tx, corr, p1w, p2t, e4s, e4r,
+    xb, gb, st, outb, us, fs, into, back, row, rs, rn, sn, rc, sc, pk, gath, plw, qw, r4, r8, small, ct_v, tt, tx, corr, p1w, p2t, e4s, e4r,
     in_sem, out_sem, s_snd, s_rcv, n_snd, n_rcv, c_snd, c_rcv, g_snd, g_rcv,
     q_snd, q_rcv, w_snd, w_rcv, r4_snd, r4_rcv, r8_snd, r8_rcv, e4_snd, e4_rcv,
 ):
@@ -64,9 +71,9 @@
     loads = {"st": pltpu.make_async_copy(st_in, st, in_sem.at[6])}
     for c in range(3):
         loads["u", c] = pltpu.make_async_copy(
-            u_in.at[c], xb.at[0, c, 0, pl.ds(O, HS), pl.ds(0, HN)], in_sem.at[c]
+            u_in.at[c], us.at[c], in_sem.at[c]
         )
-        loads["f", c] = pltpu.make_async_copy(f_in.at[c], gb.at[c, pl.ds(O, HS)], in_sem.at[3 + c])
+        loads["f", c] = pltpu.make_async_copy(f_in.at[c], fs.at[c], in_sem.at[3 + c])
     for k, ref in enumerate((p_hbm, ap_hbm, inj_hbm)):
         loads["small", k] = pltpu.make_async_copy(ref, small.at[k], in_sem.at[7 + k])
         loads["small", k].start()
@@ -109,18 +116,28 @@
     zrow = jnp.zeros((24, DIP), F32)
 
     def clear(i, carry):
+        at = jnp.where(i < O, i, i + HS)
         for c in range(3):
             for rd in range(2):
-                lo = i
                 for pp in range(2):
-                    xb[rd, c, pp, jnp.where(lo < 4, lo + 1 - pp, lo + 9 + pp)] = zrow
-            gb[c, jnp.where(i < 4, i + 1, i + 9)] = jnp.zeros((HN, DIP), F32)
+                    xb[rd, c, pp, at] = zrow
+            gb[c, at] = jnp.zeros((HN, DIP), F32)
+        return carry
+
+    lax.fori_loop(0, 10, clear, 0)
+
+    def clear_own(i, carry):
         for c in range(3):
             for rd in range(2):
                 xb[rd, c, 0, O + i, pl.ds(16, 8), :] = jnp.zeros((8, DIP), F32)
         return carry
 
-    lax.fori_loop(0, 8, clear, 0)
+    lax.fori_loop(0, HS, clear_own, 0)
+
+    d0 = lax.broadcasted_iota(jnp.int32, (DIP, DIP), 0)
+    d1 = lax.broadcasted_iota(jnp.int32, (DIP, DIP), 1)
+    into[...] = jnp.where(d0 == 4 * (d1 % LANES) + d1 // LANES, 1.0, 0.0).astype(jnp.bfloat16)
+    back[...] = jnp.where(d1 == 4 * (d0 % LANES) + d0 // LANES, 1.0, 0.0).astype(jnp.bfloat16)
 
     for a, w in ((-1, 0), (1, 1)):
         @pl.when(jnp.logical_not(has_s[a]))
@@ -180,12 +197,16 @@
     @pl.when(is_a)
     def _():
         for i in range(HS):
-            qw[0, 2, i : i + 1, :] = 0.5 * st[i, HN - 1 : HN, :]
+            row[i : i + 1, :] = 0.5 * st[i, HN - 1 : HN, :]
 
     @pl.when(is_b)
     def _():
         for i in range(HS):
-            qw[0, 2, i : i + 1, :] = 0.5 * st[i, 0:1, :]
+            row[i : i + 1, :] = 0.5 * st[i, 0:1, :]
+
+    @pl.when(is_i)
+    def _():
+        qw[0, 2] = shuffle(row[...], into[...])
 
     def row_copies(buf, snd, rcv, first, last, src):
         out = []
@@ -253,10 +274,10 @@
                 return [[xb[rd, c, src, i, t * 8 : t * 8 + 8, cols(j)] for j in range(NJ)] for t in range(3)]
 
             def pair(m, inner):
-                base = O - k + 2 * m
-                rows = [get(base - 1 + r) for r in range(2 + 2)]
+                base = O - k - lax.rem(k, 2) + 4 * m
+                rows = [get(base - 1 + r) for r in range(4 + 2)]
                 vals = {}
-                for r in range(2):
+                for r in range(4):
                     i = base + r
                     xm, x, xp = rows[r : r + 3]
                     ok = jnp.logical_and(
@@ -288,7 +309,7 @@
                     xb[rd, c, dst, base + r, t * 8 : t * 8 + 8, cols(j)] = val
                 return inner
 
-            lax.fori_loop(0, HS // 2 + k, pair, 0)
+            lax.fori_loop(0, (HS + 2 * k + 3) // 4, pair, 0)
             return carry
 
         lax.fori_loop(1, SW + 1, sweep, 0)
@@ -447,7 +468,8 @@
         k = ct * (width * width * width) / 12.0
         base = 0.5 * p - opening + inj
         k_up, k_dn = rows_sums(k)
-        k_l, k_r = lane_sums(k, first, last)
+        k_l, k_r = lane_shifts(k)
+        k_l, k_r = jnp.where(first, 0.0, k_l), jnp.where(last, 0.0, k_r)
         f_up, f_dn, f_l, f_r = [0.5 * (k + v) for v in (k_up, k_dn, k_l, k_r)]
         rden = jnp.where(valid, 1.0 / (0.5 + (f_up + f_dn + f_l + f_r)), 0.0)
         base = base * rden
@@ -456,7 +478,8 @@
         f_r = jnp.where(last, 0.0, f_r * rden)
         for _ in range(SW_L):
             p_up, p_dn = rows_sums(p)
-            p = base + f_up * p_up + f_dn * p_dn + f_l * pltpu.roll(p, 1, 1) + f_r * pltpu.roll(p, DIP - 1, 1)
+            p_l, p_r = lane_shifts(p)
+            p = (base + (f_up * p_up + f_dn * p_dn)) + (f_l * p_l + f_r * p_r)
         return p
 
     sign = jnp.where(is_b, 1.0, -1.0)
@@ -464,12 +487,9 @@
     for c in order:
         loads["f", c].wait()
 
-        def scale(i, carry, c=c):
-            gb[c, O + i] = gb[c, O + i] * st[i]
-            return carry
-
-        lax.fori_loop(0, HS, scale, 0)
+        gb[c, pl.ds(O, HS)] = shuffle((fs[c] * st[...]).reshape(HS * HN, DIP), into[...]).reshape(HS, HN, DIP)
         loads["u", c].wait()
+        xb[0, c, 0, pl.ds(O, HS), pl.ds(0, HN)] = shuffle(us[c].reshape(HS * HN, DIP), into[...]).reshape(HS, HN, DIP)
         sweeps(0, c)
         send(0, c)
 
@@ -486,6 +506,7 @@
                     piece = pltpu.roll(tiles[m], shift, 1) if shift else tiles[m]
                     val = piece if val is None else jnp.where(lane >= 32 * m, piece, val)
                 plw[2, kind, :, cols(big)] = val
+        plw[2] = shuffle(plw[2].reshape(32, DIP), into[...]).reshape(4, 8, DIP)
         send_rows(w_copies)
         get_rows(q_copies)
         get_rows(w_copies)
@@ -570,6 +591,7 @@
             put_rows(lambda i, r: outb[1, i, r : r + 1, :], put_r8)
             pl.when(is_i)(lambda: send_rows(r8_copies))
             own_tile(lambda i, r: outb[1, i, r : r + 8, :], put_out)
+        outb[c] = shuffle(outb[c].reshape(HS * HN, DIP), back[...]).reshape(HS, HN, DIP)
         copies_out[c].start()
 
     e4_copies = []
@@ -593,7 +615,8 @@
 
         def across(x):
             up, dn = rows_sums(x)
-            left, right = lane_sums(x, first, last)
+            left, right = lane_shifts(x)
+            left, right = jnp.where(first, 0.0, left), jnp.where(last, 0.0, right)
             return 0.1 * ((up + dn) + (left + right))
 
         force = flat(p1w[...]) * (flat(qw[0]) + flat(qw[1]))
@@ -607,8 +630,9 @@
         p2 = lubricate(
             opening, flat(p1w[1:4]), flat(plw[1:4, 1]), flat(plw[1:4, 2]), flat(plw[1:4, 3]), -8
         )
+        p2 = shuffle(p2[8:16], back[...])
         for j in range(NJ):
-            p2t[j] = p2[8:16, cols(j)]
+            p2t[j] = p2[:, cols(j)]
         for i in range(NN // 2):
             shift = -(i % 4) * 32 % LANES
             tile = p2t[side * 2 + i // 4]
@@ -624,7 +648,7 @@
             device_id=(s, NN - 1 - n), device_id_type=MESH,
         ).wait_recv()
 
-    p_out[...] = e4r[:, 0:32]
+    p_out[...] = e4r[...]
 
     for copy in copies_out:
         copy.wait()
@@ -655,6 +679,11 @@
         buf(3, 18, HN, DIP),
         buf(HS, HN, DIP),
         buf(3, HS, HN, DIP),
+        buf(3, HS, HN, DIP),
+        buf(3, HS, HN, DIP),
+        pltpu.VMEM((DIP, DIP), jnp.bfloat16),
+        pltpu.VMEM((DIP, DIP), jnp.bfloat16),
+        buf(8, DIP),
         buf(2, 3, 2, 4, HN, DIP),
         buf(2, 3, 2, 4, 8, DIP),
         buf(2, 3, 2, 4, 8, DIP),
@@ -682,11 +711,11 @@
         dma((2, 5)), dma((2, 5)), dma((5,)), dma((5,)), dma((2, 5)), dma((2, 5)), dma((2, 3)), dma((2, 3)),
         dma((NN // 2,)), dma,
     ]
-    return pl.pallas_call(
+    u, tile = pl.pallas_call(
         kernel,
         out_shape=(
             jax.ShapeDtypeStruct((3, HS, HN, DIP), F32),
-            jax.ShapeDtypeStruct((8, 32), F32),
+            jax.ShapeDtypeStruct((8, LANES), F32),
         ),
         in_specs=[hbm] * 7,
         out_specs=(hbm, vm),
@@ -696,6 +725,7 @@
         ),
         cost_estimate=pl.CostEstimate(flops=60_000_000, bytes_accessed=2_700_000, transcendentals=40_000),
     )(displacement, body_force, stiffness, aperture_base, contact_open, pressure_init, injection)
+    return u, tile[:, : HN * 2]
 
 
 def solution(mesh):

time: 52.8 us -> 45.3 us (0.86)
  Pallas kernels: 49.3 us -> 41.8 us
    pallas_call x1, Pallas kernels: 49.3 us -> 41.8 us  [body(): pl.pallas_call(kernel, out_shape=(jax.ShapeDtypeStruct((3, HS, HN, DIP),...]
where the time goes in v3:
time: 45.3 us; the launch traced here: 45.1 us
  Pallas kernels  41.8 us (92%)
  local copies, waits for them, and re-layouts  2.69 us (6%)
  between operations  0.65 us (1%)
    pallas_call x1, Pallas kernels, body(): pl.pallas_call(kernel, out_shape=(jax.ShapeDtypeStruct((3, HS, HN, DIP),...  41.8 us
    unnamed x4, local copies, waits for them, and re-layouts  2.69 us

profile of v3, /device:TPU:1, one launch (start us, length us, event | category | flops | bytes accessed | tf_op | source)
XLA Modules:
  0.0 45.1 jit_solution(9837416370725520826)
XLA Ops:
  0.6 41.8 %shard_map.86 = (f32[3,8,16,512]{3,2,1,0:T(8,128)}, f32[8,128]{1,0:T(8,128)}) custom-call(f32[3,8,16,512]{3,2,1,0:T(8,128)} %u_in.1, f32[3,8,16,512]{3,2,1,0:T(8,128)} %f_in.1, f32[8,16,512]{2,1,0:T(8,128)} %st_in.1, f32[8,32]{1,0:T(8,128)} %ap_hbm.1, s32[8,32]{1,0:T(8,128)} %ct_hbm.1, f32[8,32]{1,0:T(8,128)} %p_hbm.1, f32[8,32]{1,0:T(8,128)} %inj_hbm.1), custom_call_target="tpu_custom_call" | custom-call | flops 60000000 | bytes 2700000 | tf_op jit(solution)/shard_map/pallas_call | solution.py:714
  42.4 0.0 copy-start
  42.4 2.1 %copy.11 = f32[3,8,16,512]{3,2,1,0:T(8,128)} copy(f32[3,8,16,512]{3,2,1,0:T(8,128)} %get-tuple-element.8) | data formatting | bytes 1572864
  44.5 0.0 copy-done
  44.5 0.6 %copy.12 = f32[8,32]{1,0:T(8,128)} copy(f32[8,32]{1,0:T(8,128)S(1)} %bitcast.1) | data formatting | bytes 2048
Async XLA Ops:
  42.4 2.1 %copy-start = (f32[8,128]{1,0:T(8,128)S(1)}, f32[8,128]{1,0:T(8,128)}, u32[]{:S(2)}) copy-start(f32[8,128]{1,0:T(8,128)} %get-tuple-element.5) | copy-start | bytes 12292

commit v4 on v3

--- a/solution.py
+++ b/solution.py
@@ -51,9 +51,9 @@
 def kernel(
     u_in, f_in, st_in, ap_hbm, ct_hbm, p_hbm, inj_hbm,
     u_out, p_out,
-    xb, gb, st, outb, us, fs, into, back, row, rs, rn, sn, rc, sc, pk, gath, plw, qw, r4, r8, small, ct_v, tt, tx, corr, p1w, p2t, e4s, e4r,
+    xb, gb, st, outb, us, fs, into, back, row, rs, rn, sn, rc, sc, pk, gath, plw, qx, eb, eg, ea, ra, sw, c4w, c8w, small, ct_v, tt, tx, corr, p1w, p2t, e4s, e4r,
     in_sem, out_sem, s_snd, s_rcv, n_snd, n_rcv, c_snd, c_rcv, g_snd, g_rcv,
-    q_snd, q_rcv, w_snd, w_rcv, r4_snd, r4_rcv, r8_snd, r8_rcv, e4_snd, e4_rcv,
+    q_snd, q_rcv, w_snd, w_rcv, a_snd, a_rcv, b_snd, b_rcv, e4_snd, e4_rcv,
 ):
     s = lax.axis_index("strike")
     n = lax.axis_index("normal")
@@ -104,14 +104,11 @@
     for other in range(NN):
         count += greet(jnp.logical_and(is_i, n != other), (s, other))
 
-    def in_range(j):
-        return jnp.logical_and(s + (j - 2) >= 0, s + (j - 2) <= NS - 1)
-
-    for j in range(5):
-        ok = jnp.logical_and(is_i, in_range(j))
-        if j != 2:
-            count += greet(ok, (s + (j - 2), n))
-        count += greet(ok, (s + (j - 2), NN - 1 - n))
+    def near(d):
+        return jnp.logical_and(s + d >= 0, s + d <= NS - 1)
+
+    for d in (-3, -2, 2, 3):
+        count += greet(jnp.logical_and(is_i, near(d)), (s + d, n))
 
     zrow = jnp.zeros((24, DIP), F32)
 
@@ -156,21 +153,39 @@
     @pl.when(is_i)
     def _():
         tx[...] = jnp.zeros_like(tx)
-        for j in range(5):
-            @pl.when(jnp.logical_not(in_range(j)))
+        eb[...] = jnp.zeros_like(eb)
+        eg[...] = jnp.zeros_like(eg)
+        for d in range(-3, 4):
+            @pl.when(jnp.logical_not(near(d)))
             def _():
-                plw[j] = jnp.zeros((4, 8, DIP), F32)
-                qw[:, j] = jnp.zeros((2, 8, DIP), F32)
-                r4[:, j] = jnp.zeros((2, 8, DIP), F32)
-                if 1 <= j <= 3:
-                    r8[:, j - 1] = jnp.zeros((2, 8, DIP), F32)
-
-    for k in range(3):
-        loads["small", k].wait()
-    loads["ct"].wait()
-    pk[...] = jnp.concatenate([small[0], small[1], ct_v[...].astype(F32), small[2]], axis=1)
-
-    pl.semaphore_wait(barrier, count)
+                plw[d + 3] = jnp.zeros((6, 8, DIP), F32)
+                if -2 <= d <= 2:
+                    sw[d + 2] = jnp.zeros((2, 8, DIP), F32)
+                if -1 <= d <= 1:
+                    ra[:, d + 1] = jnp.zeros((2, 2, 8, DIP), F32)
+
+    loads["st"].wait()
+
+    def recip(i, carry):
+        st[i] = 0.1 / st[i]
+        return carry
+
+    lax.fori_loop(0, HS, recip, 0)
+
+    @pl.when(is_a)
+    def _():
+        for i in range(HS):
+            row[i : i + 1, :] = 0.5 * st[i, HN - 1 : HN, :]
+
+    @pl.when(is_b)
+    def _():
+        for i in range(HS):
+            row[i : i + 1, :] = 0.5 * st[i, 0:1, :]
+
+    @pl.when(is_i)
+    def _():
+        qx[0] = shuffle(row[...], into[...])
+
 
     gathers = []
     for k, mid in enumerate((NN // 2 - 1, NN // 2)):
@@ -183,83 +198,57 @@
                 ),
             )
         )
-    for cond, copy in gathers:
-        pl.when(cond)(copy.start)
-
-    loads["st"].wait()
-
-    def recip(i, carry):
-        st[i] = 0.1 / st[i]
-        return carry
-
-    lax.fori_loop(0, HS, recip, 0)
-
-    @pl.when(is_a)
-    def _():
-        for i in range(HS):
-            row[i : i + 1, :] = 0.5 * st[i, HN - 1 : HN, :]
-
-    @pl.when(is_b)
-    def _():
-        for i in range(HS):
-            row[i : i + 1, :] = 0.5 * st[i, 0:1, :]
-
-    @pl.when(is_i)
-    def _():
-        qw[0, 2] = shuffle(row[...], into[...])
-
-    def row_copies(buf, snd, rcv, first, last, src):
-        out = []
+
+    q_copy = pltpu.make_async_remote_copy(
+        src_ref=qx.at[0], dst_ref=qx.at[1], send_sem=q_snd, recv_sem=q_rcv,
+        device_id=(s, NN - 1 - n), device_id_type=MESH,
+    )
+
+    def pair_of(src, dst_there, dst_here, snd, rcv_there, rcv_here, target):
+        return [
+            pltpu.make_async_remote_copy(
+                src_ref=src, dst_ref=dst, send_sem=snd, recv_sem=rcv, device_id=target, device_id_type=MESH
+            )
+            for dst, rcv in ((dst_there, rcv_there), (dst_here, rcv_here))
+        ]
+
+    a_copies, b_copies, w_copies = [], [], []
+    for d in (-1, 1, 0):
         for rel in range(2):
-            for j in range(first, last):
-                if rel == 0 and j == 2:
-                    continue
-                target_n = n if rel == 0 else NN - 1 - n
-                snd_copy = pltpu.make_async_remote_copy(
-                    src_ref=src, dst_ref=buf.at[rel, 4 - j - first], send_sem=snd.at[rel, j - first],
-                    recv_sem=rcv.at[rel, 4 - j - first], device_id=(s + (j - 2), target_n), device_id_type=MESH,
+            if d == 0 and rel == 0:
+                continue
+            a_copies.append(
+                [near(d)] + pair_of(
+                    ea.at[1 + d], ra.at[rel, 1 - d], ra.at[rel, 1 + d], a_snd.at[rel, 1 + d],
+                    a_rcv.at[rel, 1 - d], a_rcv.at[rel, 1 + d], (s + d, n if rel == 0 else NN - 1 - n),
                 )
-                rcv_copy = pltpu.make_async_remote_copy(
-                    src_ref=src, dst_ref=buf.at[rel, j - first], send_sem=snd.at[rel, j - first],
-                    recv_sem=rcv.at[rel, j - first], device_id=(s + (j - 2), target_n), device_id_type=MESH,
-                )
-                out.append((in_range(j), snd_copy, rcv_copy))
-        return out
-
-    q_copies = row_copies(qw, q_snd, q_rcv, 0, 5, qw.at[0, 2])
-    r4_copies = row_copies(r4, r4_snd, r4_rcv, 0, 5, r4.at[0, 2])
-    r8_copies = row_copies(r8, r8_snd, r8_rcv, 1, 4, r8.at[0, 1])
-    w_copies = []
-    for j in (0, 1, 3, 4):
+            )
+    for d in (-2, 2, -1, 1):
+        b_copies.append(
+            [near(d)] + pair_of(
+                sw.at[2], sw.at[2 - d], sw.at[2 + d], b_snd.at[2 + d], b_rcv.at[2 - d], b_rcv.at[2 + d], (s + d, n)
+            )
+        )
+    for d, kinds in ((-3, 2), (3, 2), (-2, 5), (2, 5), (-1, 6), (1, 6)):
+        part = pl.ds(0, kinds)
         w_copies.append(
-            (
-                in_range(j),
-                pltpu.make_async_remote_copy(
-                    src_ref=plw.at[2], dst_ref=plw.at[4 - j], send_sem=w_snd.at[j], recv_sem=w_rcv.at[4 - j],
-                    device_id=(s + (j - 2), n), device_id_type=MESH,
-                ),
-                pltpu.make_async_remote_copy(
-                    src_ref=plw.at[2], dst_ref=plw.at[j], send_sem=w_snd.at[j], recv_sem=w_rcv.at[j],
-                    device_id=(s + (j - 2), n), device_id_type=MESH,
-                ),
+            [near(d)] + pair_of(
+                plw.at[3, part], plw.at[3 - d, part], plw.at[3 + d, part], w_snd.at[3 + d],
+                w_rcv.at[3 - d], w_rcv.at[3 + d], (s + d, n),
             )
         )
 
-    def send_rows(copies):
+    def send_all(copies):
         for cond, snd, _ in copies:
             pl.when(cond)(snd.start)
 
-    def get_rows(copies):
+    def get_all(copies):
         for cond, _, rcv in copies:
             pl.when(cond)(rcv.wait_recv)
 
-    def end_rows(copies):
+    def end_all(copies):
         for cond, snd, _ in copies:
             pl.when(cond)(snd.wait_send)
-
-    @pl.when(is_i)
-    def _():
-        send_rows(q_copies)
 
     keep_hi = jnp.logical_or(has_n[1], sub >= 4)
     keep_lo = jnp.logical_or(has_n[-1], sub < 4)
@@ -435,27 +424,42 @@
             above = jnp.where(is_b, own, far)
             tt[r + 3] = jnp.where(sub5 == 3, -below, jnp.where(sub5 == 4, above, 0.0))
 
-        def tile_sweep(src, dst, lo, hi, shift):
-            def one(i, carry):
-                x = [src[i, :, cols(j)] for j in range(NJ)]
-                left, right = lane_pair(x, lane)
-                for j in range(NJ):
-                    sy = pltpu.roll(x[j], 1, 0) + pltpu.roll(x[j], 7, 0)
-                    sx = src[i - 1, :, cols(j)] + src[i + 1, :, cols(j)]
-                    dst[i - shift, :, cols(j)] = (
-                        0.2 * (x[j] + sy) + 0.1 * (sx + left[j] + right[j]) + tt[i, :, cols(j)]
+        def tile_sweep(src, dst, first, trips, shift):
+            def four(m, carry):
+                base = first + 4 * m
+                rows = [[src[base - 1 + r, :, cols(j)] for j in range(NJ)] for r in range(6)]
+                vals = {}
+                for r in range(4):
+                    i = base + r
+                    xm, x, xp = rows[r : r + 3]
+                    ok = jnp.logical_and(
+                        jnp.logical_or(has_s[-1], i >= 3), jnp.logical_or(has_s[1], i < 3 + HS)
                     )
+                    one, two = jnp.where(ok, 0.1, 0.0), jnp.where(ok, 0.2, 0.0)
+                    left, right = lane_pair(x, lane)
+                    for j in range(NJ):
+                        sy = pltpu.roll(x[j], 1, 0) + pltpu.roll(x[j], 7, 0)
+                        vals[r, j] = (
+                            two * (x[j] + sy) + one * ((xm[j] + xp[j]) + (left[j] + right[j]))
+                            + tt[i, :, cols(j)]
+                        )
+                for (r, j), val in vals.items():
+                    dst[base + r - shift, :, cols(j)] = val
                 return carry
 
-            lax.fori_loop(jnp.where(has_s[-1], lo, 3), jnp.where(has_s[1], hi, 11), one, 0)
-
-        tile_sweep(tt, tx.at[0], 1, 13, 0)
-        tile_sweep(tx.at[0], tx.at[1], 2, 12, 0)
-        tile_sweep(tx.at[1], corr, 3, 11, 3)
-
-    def win_row(ref, r):
-        j, i = divmod(r + 16, 8)
+            lax.fori_loop(0, trips, four, 0)
+
+        tile_sweep(tt, tx.at[0], 1, 3, 0)
+        tile_sweep(tx.at[0], tx.at[1], 1, 3, 0)
+        tile_sweep(tx.at[1], corr, 3, 2, 3)
+
+    def win_row(ref, r, half):
+        j, i = divmod(r + 8 * half, 8)
         return ref(j)[i : i + 1, :]
+
+    def q_row(rel, r):
+        own = win_row(lambda j: plw[j, 5], r, 3)
+        return own if rel == 0 else win_row(lambda j: plw[j, 1], r, 3) - own
 
     def lubricate(opening, p, ap, ct, inj, first_row):
         rows = opening.shape[0]
@@ -484,35 +488,160 @@
 
     sign = jnp.where(is_b, 1.0, -1.0)
 
-    for c in order:
+    def antisymmetric():
+        near_row = pl.multiple_of(jnp.where(is_b, 0, 8), 8)
+        far_row = pl.multiple_of(jnp.where(is_b, 8, 0), 8)
+        c_up, c_dn = jnp.where(is_b, -1.0, 0.0), jnp.where(is_b, 0.0, -1.0)
+        for i in range(HS):
+            eb[0, 9 + i] = xb[0, 1, 0, O + i, pl.ds(near_row, 8), :]
+            eg[9 + i] = gb[1, O + i, pl.ds(near_row, 8), :]
+
+        def sweep(k, carry):
+            src, dst = lax.rem(k - 1, 2), lax.rem(k, 2)
+
+            def four(m, inner):
+                base = jnp.where(k <= 4, 5, 1) + 8 * m
+                rows = [[eb[src, base - 1 + r, :, cols(j)] for j in range(NJ)] for r in range(10)]
+                vals = {}
+                for r in range(8):
+                    i = base + r
+                    xm, x, xp = rows[r : r + 3]
+                    ok = jnp.logical_and(
+                        jnp.logical_or(has_s[-1], i >= 9), jnp.logical_or(has_s[1], i < 9 + HS)
+                    )
+                    one, two = jnp.where(ok, 0.1, 0.0), jnp.where(ok, 0.2, 0.0)
+                    left, right = lane_pair(x, lane)
+                    for j in range(NJ):
+                        up = jnp.where(sub == 0, c_up * x[j], pltpu.roll(x[j], 1, 0))
+                        dn = jnp.where(sub == 7, c_dn * x[j], pltpu.roll(x[j], 7, 0))
+                        vals[r, j] = (
+                            two * (x[j] + (up + dn)) + one * ((xm[j] + xp[j]) + (left[j] + right[j]))
+                            + eg[i, :, cols(j)]
+                        )
+                for (r, j), val in vals.items():
+                    eb[dst, base + r, :, cols(j)] = val
+                return inner
+
+            lax.fori_loop(0, jnp.where(k <= 4, 2, 3), four, 0)
+            return carry
+
+        def take(e):
+            for cond, row_at in ((is_a, 7), (is_b, 0)):
+                @pl.when(cond)
+                def _():
+                    for i in range(24):
+                        ea[i // 8, e, i % 8 : i % 8 + 1, :] = eb[0, 1 + i, row_at : row_at + 1, :]
+
+        lax.fori_loop(1, 2, sweep, 0)
+        for i in range(HS):
+            far = xb[0, 1, 0, O + i, pl.ds(far_row, 8), :]
+            from_far = jnp.where(is_b, pltpu.roll(far, 7, 0), pltpu.roll(far, 1, 0))
+            eb[1, 9 + i] = eb[1, 9 + i] + jnp.where(sub5 == jnp.where(is_b, 7, 0), 0.2 * from_far, 0.0)
+        lax.fori_loop(2, 5, sweep, 0)
+        take(0)
+        lax.fori_loop(5, 9, sweep, 0)
+        take(1)
+        ra[0, 1] = ea[1]
+
+    def flat(x):
+        return x.reshape(x.shape[0] * 8, DIP)
+
+    def spread(rows, first_row):
+        lanes = lax.broadcasted_iota(jnp.int32, (rows, DIP), 1)
+        first, last = lanes == 0, lanes == DIP - 1
+        strike = lax.broadcasted_iota(jnp.int32, (rows, DIP), 0) + (s * HS + first_row)
+        valid = jnp.logical_and(strike >= 0, strike < NS * HS)
+
+        def across(x):
+            up, dn = rows_sums(x)
+            left, right = lane_shifts(x)
+            left, right = jnp.where(first, 0.0, left), jnp.where(last, 0.0, right)
+            return 0.1 * ((up + dn) + (left + right))
+
+        return across, valid
+
+    def layers(d, force, k, across, valid):
+        out = []
+        for m in range(min(k, 9 - k)):
+            here = d[m] if m < len(d) else None
+            val = None
+            if here is not None:
+                val = across(here)
+                if m > 0:
+                    val = val + 0.2 * here
+            if m + 1 < len(d):
+                val = val + 0.2 * d[m + 1]
+            if m > 0:
+                below = 0.2 * d[m - 1]
+                val = below if val is None else val + below
+            if m == 0 and force is not None:
+                val = force if val is None else val + force
+            out.append(jnp.where(valid, val, 0.0))
+        return out
+
+    def early():
+        across, valid = spread(56, -24)
+        force = flat(plw[:, 0]) * flat(plw[:, 1])
+        d = [force]
+        for k in range(2, 5):
+            d = layers(d, force, k, across, valid)
+        d = [x[8:48] for x in d]
+        c4w[...] = d[0].reshape(5, 8, DIP)
+        across, valid = spread(40, -16)
+        for k in range(5, 9):
+            d = layers(d, None, k, across, valid)
+        c8w[...] = d[0][8:32].reshape(3, 8, DIP)
+
+    def ready(c):
         loads["f", c].wait()
-
         gb[c, pl.ds(O, HS)] = shuffle((fs[c] * st[...]).reshape(HS * HN, DIP), into[...]).reshape(HS, HN, DIP)
         loads["u", c].wait()
         xb[0, c, 0, pl.ds(O, HS), pl.ds(0, HN)] = shuffle(us[c].reshape(HS * HN, DIP), into[...]).reshape(HS, HN, DIP)
-        sweeps(0, c)
-        send(0, c)
-
-    @pl.when(is_i)
-    def _():
-        gath[n] = pk[...]
-        pltpu.make_async_copy(gath.at[pl.ds(0, NN - 1)], gath.at[pl.ds(0, NN - 1)], g_rcv).wait()
-        for big in range(NJ):
-            tiles = [gath[big * 4 + m] for m in range(4)]
-            for kind in range(4):
-                val = None
-                for m in range(4):
-                    shift = (m - kind) % 4 * 32
-                    piece = pltpu.roll(tiles[m], shift, 1) if shift else tiles[m]
-                    val = piece if val is None else jnp.where(lane >= 32 * m, piece, val)
-                plw[2, kind, :, cols(big)] = val
-        plw[2] = shuffle(plw[2].reshape(32, DIP), into[...]).reshape(4, 8, DIP)
-        send_rows(w_copies)
-        get_rows(q_copies)
-        get_rows(w_copies)
-        traction(
-            lambda r: win_row(lambda j: plw[j, 0], r), lambda rel, r: win_row(lambda j: qw[rel, j], r)
-        )
+
+    for k in range(3):
+        loads["small", k].wait()
+    loads["ct"].wait()
+    pk[...] = jnp.concatenate([small[0], small[1], ct_v[...].astype(F32), small[2]], axis=1)
+
+    def unpack():
+        @pl.when(is_i)
+        def _():
+            gath[n] = pk[...]
+            pltpu.make_async_copy(gath.at[pl.ds(0, NN - 1)], gath.at[pl.ds(0, NN - 1)], g_rcv).wait()
+            for big in range(NJ):
+                tiles = [gath[big * 4 + m] for m in range(4)]
+                for kind, place in enumerate((0, 2, 3, 4)):
+                    val = None
+                    for m in range(4):
+                        shift = (m - kind) % 4 * 32
+                        piece = pltpu.roll(tiles[m], shift, 1) if shift else tiles[m]
+                        val = piece if val is None else jnp.where(lane >= 32 * m, piece, val)
+                    plw[3, place, :, cols(big)] = val
+            both = shuffle(jnp.concatenate([plw[3, 0], plw[3, 2], plw[3, 3], plw[3, 4]], axis=0), into[...])
+            for m, place in enumerate((0, 2, 3, 4)):
+                plw[3, place] = both[8 * m : 8 * m + 8]
+            q_copy.wait_recv()
+            plw[3, 1] = qx[0] + qx[1]
+            plw[3, 5] = qx[0]
+            send_all(w_copies)
+
+    def total():
+        @pl.when(is_i)
+        def _():
+            get_all(a_copies)
+            for e in range(2):
+                own = ra[0, 0, e] + ra[0, 1, e] + ra[0, 2, e]
+                sw[2, e] = sign * (own - (ra[1, 0, e] + ra[1, 1, e] + ra[1, 2, e]))
+            send_all(b_copies)
+
+    def pressed():
+        @pl.when(is_i)
+        def _():
+            get_all(w_copies)
+            traction(lambda r: win_row(lambda j: plw[j, 0], r, 3), q_row)
+            early()
+
+    sign = jnp.where(is_b, 1.0, -1.0)
 
     def to_second(c):
         def store(i, low, high):
@@ -539,60 +668,11 @@
             for i in range(HS):
                 put(i, 0, get(i, 0) + jnp.where(r4sub, pltpu.roll(corr[i], 4, 0), 0.0))
 
-    def put_rows(get, put):
-        @pl.when(is_a)
-        def _():
-            for i in range(HS):
-                put(i, get(i, HN - 1))
-
-        @pl.when(is_b)
-        def _():
-            for i in range(HS):
-                put(i, get(i, 0))
-
     def put_second(i, r, v):
         xb[1, 1, 0, O + i, r : r + 8, :] = v
 
     def put_out(i, r, v):
         outb[1, i, r : r + 8, :] = v
-
-    def put_r4(i, v):
-        r4[0, 2, i : i + 1, :] = v
-
-    def put_r8(i, v):
-        r8[0, 1, i : i + 1, :] = v
-
-    for c in order:
-        merge(0, c, to_second(c))
-        if c == 1:
-            own_tile(lambda i, r: xb[1, 1, 0, O + i, r : r + 8, :], put_second)
-            put_rows(lambda i, r: xb[1, 1, 0, O + i, r : r + 1, :], put_r4)
-            pl.when(is_i)(lambda: send_rows(r4_copies))
-        sweeps(1, c)
-        send(1, c)
-
-    def flat(x):
-        return x.reshape(x.shape[0] * 8, DIP)
-
-    @pl.when(is_i)
-    def _():
-        get_rows(r4_copies)
-        opening = sign * (flat(r4[0]) - flat(r4[1]))
-        p1 = lubricate(opening, *[flat(plw[:, kind]) for kind in range(4)], -16)
-        p1w[...] = p1.reshape(5, 8, DIP)
-        traction(
-            lambda r: win_row(lambda j: p1w[j], r), lambda rel, r: win_row(lambda j: qw[rel, j], r)
-        )
-
-    copies_out = [pltpu.make_async_copy(outb.at[c], u_out.at[c], out_sem.at[c]) for c in range(3)]
-    for c in order:
-        merge(1, c, to_out(c))
-        if c == 1:
-            put_rows(lambda i, r: outb[1, i, r : r + 1, :], put_r8)
-            pl.when(is_i)(lambda: send_rows(r8_copies))
-            own_tile(lambda i, r: outb[1, i, r : r + 8, :], put_out)
-        outb[c] = shuffle(outb[c].reshape(HS * HN, DIP), back[...]).reshape(HS, HN, DIP)
-        copies_out[c].start()
 
     e4_copies = []
     for i in range(NN // 2):
@@ -606,40 +686,82 @@
             )
         )
 
-    @pl.when(is_i)
-    def _():
-        lanes = lax.broadcasted_iota(jnp.int32, (40, DIP), 1)
-        first, last = lanes == 0, lanes == DIP - 1
-        strike = lax.broadcasted_iota(jnp.int32, (40, DIP), 0) + (s * HS - 16)
-        valid = jnp.logical_and(strike >= 0, strike < NS * HS)
-
-        def across(x):
-            up, dn = rows_sums(x)
-            left, right = lane_shifts(x)
-            left, right = jnp.where(first, 0.0, left), jnp.where(last, 0.0, right)
-            return 0.1 * ((up + dn) + (left + right))
-
-        force = flat(p1w[...]) * (flat(qw[0]) + flat(qw[1]))
-        d0 = jnp.where(valid, across(force) + force, 0.0)
-        d1 = 0.2 * force
-        e0 = jnp.where(valid, 0.2 * d1 + across(d0) + force, 0.0)
-        e1 = jnp.where(valid, 0.2 * d1 + across(d1) + 0.2 * d0, 0.0)
-        extra = (0.2 * e1 + across(e0) + force)[8:32]
-        get_rows(r8_copies)
-        opening = sign * (flat(r8[0]) - flat(r8[1])) + extra
-        p2 = lubricate(
-            opening, flat(p1w[1:4]), flat(plw[1:4, 1]), flat(plw[1:4, 2]), flat(plw[1:4, 3]), -8
-        )
-        p2 = shuffle(p2[8:16], back[...])
-        for j in range(NJ):
-            p2t[j] = p2[:, cols(j)]
-        for i in range(NN // 2):
-            shift = -(i % 4) * 32 % LANES
-            tile = p2t[side * 2 + i // 4]
-            e4s[i] = pltpu.roll(tile, shift, 1) if shift else tile
-        for cond, copy in e4_copies:
+    def plane():
+        @pl.when(is_i)
+        def _():
+            get_all(b_copies)
+            p1 = lubricate(
+                flat(sw[:, 0]) + flat(c4w[...]), *[flat(plw[1:6, kind]) for kind in (0, 2, 3, 4)], -16
+            )
+            p1w[...] = p1.reshape(5, 8, DIP)
+            across, valid = spread(40, -16)
+            force = p1 * flat(plw[1:6, 1])
+            d = layers([force], force, 2, across, valid)
+            d = layers(d, force, 6 + 1, across, valid)
+            d = layers(d, force, 8, across, valid)
+            opening = (flat(sw[1:4, 1]) + flat(c8w[...])) + d[0][8:32]
+            p2 = lubricate(opening, p1[8:32], *[flat(plw[2:5, kind]) for kind in (2, 3, 4)], -8)
+            p2 = shuffle(p2[8:16], back[...])
+            for j in range(NJ):
+                p2t[j] = p2[:, cols(j)]
+            for i in range(NN // 2):
+                shift = -(i % 4) * 32 % LANES
+                tile = p2t[side * 2 + i // 4]
+                e4s[i] = pltpu.roll(tile, shift, 1) if shift else tile
+            for cond, copy in e4_copies:
+                pl.when(cond)(copy.start)
+            e4r[...] = e4s[jnp.where(is_b, 0, 7)]
+            traction(lambda r: win_row(lambda j: p1w[j], r, 2), q_row)
+
+    def start():
+        ready(1)
+        pl.semaphore_wait(barrier, count)
+        for cond, copy in gathers:
             pl.when(cond)(copy.start)
-        e4r[...] = e4s[jnp.where(is_b, 0, 7)]
+        pl.when(is_i)(q_copy.start)
+
+    def ahead():
+        @pl.when(is_i)
+        def _():
+            antisymmetric()
+            send_all(a_copies)
+
+    def one(c):
+        if c != 1:
+            ready(c)
+        sweeps(0, c)
+        send(0, c)
+
+    def two(c):
+        merge(0, c, to_second(c))
+        if c == 1:
+            own_tile(lambda i, r: xb[1, 1, 0, O + i, r : r + 8, :], put_second)
+        sweeps(1, c)
+        send(1, c)
+
+    copies_out = [pltpu.make_async_copy(outb.at[c], u_out.at[c], out_sem.at[c]) for c in range(3)]
+    def last(c):
+        merge(1, c, to_out(c))
+        if c == 1:
+            own_tile(lambda i, r: outb[1, i, r : r + 8, :], put_out)
+        outb[c] = shuffle(outb[c].reshape(HS * HN, DIP), back[...]).reshape(HS, HN, DIP)
+        copies_out[c].start()
+
+    start()
+    ahead()
+    one(0)
+    one(2)
+    unpack()
+    one(1)
+    total()
+    two(0)
+    two(2)
+    pressed()
+    two(1)
+    plane()
+    last(0)
+    last(2)
+    last(1)
 
     @pl.when(jnp.logical_not(is_i))
     def _():
@@ -662,8 +784,9 @@
 
     @pl.when(is_i)
     def _():
-        for copies in (q_copies, w_copies, r4_copies, r8_copies):
-            end_rows(copies)
+        q_copy.wait_send()
+        for copies in (a_copies, b_copies, w_copies):
+            end_all(copies)
 
 
 def body(displacement, body_force, stiffness, aperture_base, contact_open, pressure_init, injection):
@@ -691,10 +814,15 @@
         buf(2, 3, 2, 2, 8, DIP),
         buf(8, LANES),
         buf(NN, 8, LANES),
-        buf(5, 4, 8, DIP),
-        buf(2, 5, 8, DIP),
-        buf(2, 5, 8, DIP),
-        buf(2, 3, 8, DIP),
+        buf(7, 6, 8, DIP),
+        buf(2, 8, DIP),
+        buf(2, 26, 8, DIP),
+        buf(26, 8, DIP),
+        buf(3, 2, 8, DIP),
+        buf(2, 3, 2, 8, DIP),
+        buf(5, 2, 8, DIP),
+        buf(5, 8, DIP),
+        buf(3, 8, DIP),
         buf(3, 8, 32),
         pltpu.VMEM((8, 32), jnp.int32),
         buf(14, 8, DIP),
@@ -708,7 +836,7 @@
         dma((2, 3, 2)), dma((2, 3, 2)), dma((2, 3, 2)), dma((2, 3, 2)),
         dma((2, 3, 2, 2)), dma((2, 3, 2, 2)),
         dma((2,)), dma,
-        dma((2, 5)), dma((2, 5)), dma((5,)), dma((5,)), dma((2, 5)), dma((2, 5)), dma((2, 3)), dma((2, 3)),
+        dma, dma, dma((7,)), dma((7,)), dma((2, 3)), dma((2, 3)), dma((5,)), dma((5,)),
         dma((NN // 2,)), dma,
     ]
     u, tile = pl.pallas_call(

time: 45.3 us -> 35.5 us (0.78)
  Pallas kernels: 41.8 us -> 32 us
    pallas_call x1, Pallas kernels: 41.8 us -> 32 us  [body(): pl.pallas_call(kernel, out_shape=(jax.ShapeDtypeStruct((3, HS, HN, DIP),...]
where the time goes in v4:
time: 35.5 us; the launch traced here: 35.4 us
  Pallas kernels  32 us (90%)
  local copies, waits for them, and re-layouts  2.69 us (8%)
  between operations  0.65 us (2%)
    pallas_call x1, Pallas kernels, body(): pl.pallas_call(kernel, out_shape=(jax.ShapeDtypeStruct((3, HS, HN, DIP),...  32 us
    unnamed x4, local copies, waits for them, and re-layouts  2.69 us

profile of v4, /device:TPU:1, one launch (start us, length us, event | category | flops | bytes accessed | tf_op | source)
XLA Modules:
  0.0 35.4 jit_solution(14305879072051463592)
XLA Ops:
  0.6 32.0 %shard_map.86 = (f32[3,8,16,512]{3,2,1,0:T(8,128)}, f32[8,128]{1,0:T(8,128)}) custom-call(f32[3,8,16,512]{3,2,1,0:T(8,128)} %u_in.1, f32[3,8,16,512]{3,2,1,0:T(8,128)} %f_in.1, f32[8,16,512]{2,1,0:T(8,128)} %st_in.1, f32[8,32]{1,0:T(8,128)} %ap_hbm.1, s32[8,32]{1,0:T(8,128)} %ct_hbm.1, f32[8,32]{1,0:T(8,128)} %p_hbm.1, f32[8,32]{1,0:T(8,128)} %inj_hbm.1), custom_call_target="tpu_custom_call" | custom-call | flops 60000000 | bytes 2700000 | tf_op jit(solution)/shard_map/pallas_call | solution.py:842
  32.7 0.0 copy-start
  32.7 2.1 %copy.11 = f32[3,8,16,512]{3,2,1,0:T(8,128)} copy(f32[3,8,16,512]{3,2,1,0:T(8,128)} %get-tuple-element.8) | data formatting | bytes 1572864
  34.8 0.0 copy-done
  34.8 0.6 %copy.12 = f32[8,32]{1,0:T(8,128)} copy(f32[8,32]{1,0:T(8,128)S(1)} %bitcast.1) | data formatting | bytes 2048
Async XLA Ops:
  32.7 2.1 %copy-start = (f32[8,128]{1,0:T(8,128)S(1)}, f32[8,128]{1,0:T(8,128)}, u32[]{:S(2)}) copy-start(f32[8,128]{1,0:T(8,128)} %get-tuple-element.5) | copy-start | bytes 12292

commit v5 on v4

--- a/solution.py
+++ b/solution.py
@@ -52,7 +52,7 @@
     u_in, f_in, st_in, ap_hbm, ct_hbm, p_hbm, inj_hbm,
     u_out, p_out,
     xb, gb, st, outb, us, fs, into, back, row, rs, rn, sn, rc, sc, pk, gath, plw, qx, eb, eg, ea, ra, sw, c4w, c8w, small, ct_v, tt, tx, corr, p1w, p2t, e4s, e4r,
-    in_sem, out_sem, s_snd, s_rcv, n_snd, n_rcv, c_snd, c_rcv, g_snd, g_rcv,
+    in_sem, s_snd, s_rcv, n_snd, n_rcv, c_snd, c_rcv, g_snd, g_rcv,
     q_snd, q_rcv, w_snd, w_rcv, a_snd, a_rcv, b_snd, b_rcv, e4_snd, e4_rcv,
 ):
     s = lax.axis_index("strike")
@@ -739,13 +739,11 @@
         sweeps(1, c)
         send(1, c)
 
-    copies_out = [pltpu.make_async_copy(outb.at[c], u_out.at[c], out_sem.at[c]) for c in range(3)]
     def last(c):
         merge(1, c, to_out(c))
         if c == 1:
             own_tile(lambda i, r: outb[1, i, r : r + 8, :], put_out)
-        outb[c] = shuffle(outb[c].reshape(HS * HN, DIP), back[...]).reshape(HS, HN, DIP)
-        copies_out[c].start()
+        u_out[c] = shuffle(outb[c].reshape(HS * HN, DIP), back[...]).reshape(HS, HN, DIP)
 
     start()
     ahead()
@@ -772,8 +770,6 @@
 
     p_out[...] = e4r[...]
 
-    for copy in copies_out:
-        copy.wait()
     for group in msgs.values():
         for cond, snd, _ in group:
             pl.when(cond)(snd.wait_send)
@@ -832,7 +828,7 @@
         buf(NJ, 8, LANES),
         buf(NN // 2, 8, LANES),
         buf(8, LANES),
-        dma((11,)), dma((3,)),
+        dma((11,)),
         dma((2, 3, 2)), dma((2, 3, 2)), dma((2, 3, 2)), dma((2, 3, 2)),
         dma((2, 3, 2, 2)), dma((2, 3, 2, 2)),
         dma((2,)), dma,
@@ -842,11 +838,11 @@
     u, tile = pl.pallas_call(
         kernel,
         out_shape=(
-            jax.ShapeDtypeStruct((3, HS, HN, DIP), F32),
-            jax.ShapeDtypeStruct((8, LANES), F32),
+            pltpu.VMEM((3, HS, HN, DIP), F32),
+            pltpu.VMEM((8, LANES), F32),
         ),
         in_specs=[hbm] * 7,
-        out_specs=(hbm, vm),
+        out_specs=(vm, vm),
         scratch_shapes=scratch,
         compiler_params=pltpu.CompilerParams(
             collective_id=0, has_side_effects=True, vmem_limit_bytes=60 * 2**20

time: 35.5 us -> 33.6 us (0.946)
  local copies, waits for them, and re-layouts: 2.69 us -> 1.47 us
  Pallas kernels: 32 us -> 31.4 us
    unnamed x4 -> x2, local copies, waits for them, and re-layouts: 2.69 us -> 1.47 us
    pallas_call x1, Pallas kernels: 32 us -> 31.4 us  [body(): pl.pallas_call(kernel, out_shape=(pltpu.VMEM((3, HS, HN, DIP), F32), pltp...]
where the time goes in v5:
time: 33.6 us; the launch traced here: 33.5 us
  Pallas kernels  31.4 us (93%)
  local copies, waits for them, and re-layouts  1.47 us (4%)
  between operations  0.64 us (2%)
    pallas_call x1, Pallas kernels, body(): pl.pallas_call(kernel, out_shape=(pltpu.VMEM((3, HS, HN, DIP), F32), pltp...  31.4 us
    unnamed x2, local copies, waits for them, and re-layouts  1.47 us

profile of v5, /device:TPU:1, one launch (start us, length us, event | category | flops | bytes accessed | tf_op | source)
XLA Modules:
  0.0 33.5 jit_solution(15970415855432017358)
XLA Ops:
  0.6 31.4 %shard_map.86 = (f32[3,8,16,512]{3,2,1,0:T(8,128)S(1)}, f32[8,128]{1,0:T(8,128)S(1)}) custom-call(f32[3,8,16,512]{3,2,1,0:T(8,128)} %u_in.1, f32[3,8,16,512]{3,2,1,0:T(8,128)} %f_in.1, f32[8,16,512]{2,1,0:T(8,128)} %st_in.1, f32[8,32]{1,0:T(8,128)} %ap_hbm.1, s32[8,32]{1,0:T(8,128)} %ct_hbm.1, f32[8,32]{1,0:T(8,128)} %p_hbm.1, f32[8,32]{1,0:T(8,128)} %inj_hbm.1), custom_call_target="tpu_custom_call" | custom-call | flops 60000000 | bytes 2700000 | tf_op jit(solution)/shard_map/pallas_call | solution.py:838
  32.1 0.9 %copy.11 = f32[3,8,16,512]{3,2,1,0:T(8,128)} copy(f32[3,8,16,512]{3,2,1,0:T(8,128)S(1)} %get-tuple-element.6) | data formatting | bytes 1572864
  32.9 0.6 %copy.12 = f32[8,32]{1,0:T(8,128)} copy(f32[8,32]{1,0:T(8,128)S(1)} %bitcast.1) | data formatting | bytes 2048

commit v6 on v5

--- a/solution.py
+++ b/solution.py
@@ -39,8 +39,7 @@
     rest = x - high.astype(F32)
     mid = rest.astype(jnp.bfloat16)
     low = (rest - mid.astype(F32)).astype(jnp.bfloat16)
-    out = [jnp.dot(part, matrix, preferred_element_type=F32) for part in (high, mid, low)]
-    return out[0] + (out[1] + out[2])
+    return jnp.dot(jnp.concatenate([high, mid, low], axis=1), matrix, preferred_element_type=F32)
 
 
 def rows_sums(x):
@@ -133,8 +132,11 @@
 
     d0 = lax.broadcasted_iota(jnp.int32, (DIP, DIP), 0)
     d1 = lax.broadcasted_iota(jnp.int32, (DIP, DIP), 1)
-    into[...] = jnp.where(d0 == 4 * (d1 % LANES) + d1 // LANES, 1.0, 0.0).astype(jnp.bfloat16)
-    back[...] = jnp.where(d1 == 4 * (d0 % LANES) + d0 // LANES, 1.0, 0.0).astype(jnp.bfloat16)
+    one_in = jnp.where(d0 == 4 * (d1 & (LANES - 1)) + jnp.right_shift(d1, 7), 1.0, 0.0).astype(jnp.bfloat16)
+    one_back = jnp.where(d1 == 4 * (d0 & (LANES - 1)) + jnp.right_shift(d0, 7), 1.0, 0.0).astype(jnp.bfloat16)
+    for part in range(3):
+        into[pl.ds(part * DIP, DIP)] = one_in
+        back[pl.ds(part * DIP, DIP)] = one_back
 
     for a, w in ((-1, 0), (1, 1)):
         @pl.when(jnp.logical_not(has_s[a]))
@@ -800,8 +802,8 @@
         buf(3, HS, HN, DIP),
         buf(3, HS, HN, DIP),
         buf(3, HS, HN, DIP),
-        pltpu.VMEM((DIP, DIP), jnp.bfloat16),
-        pltpu.VMEM((DIP, DIP), jnp.bfloat16),
+        pltpu.VMEM((3 * DIP, DIP), jnp.bfloat16),
+        pltpu.VMEM((3 * DIP, DIP), jnp.bfloat16),
         buf(8, DIP),
         buf(2, 3, 2, 4, HN, DIP),
         buf(2, 3, 2, 4, 8, DIP),

time: 33.6 us -> 33.6 us (level)
  no operation moved by 1% of the time
where the time goes in v6:
time: 33.6 us; the launch traced here: 33.5 us
  Pallas kernels  31.4 us (93%)
  local copies, waits for them, and re-layouts  1.47 us (4%)
  between operations  0.64 us (2%)
    pallas_call x1, Pallas kernels, body(): pl.pallas_call(kernel, out_shape=(pltpu.VMEM((3, HS, HN, DIP), F32), pltp...  31.4 us
    unnamed x2, local copies, waits for them, and re-layouts  1.47 us

profile of v6, /device:TPU:1, one launch (start us, length us, event | category | flops | bytes accessed | tf_op | source)
XLA Modules:
  0.0 33.5 jit_solution(17620470855526621571)
XLA Ops:
  0.6 31.4 %shard_map.86 = (f32[3,8,16,512]{3,2,1,0:T(8,128)S(1)}, f32[8,128]{1,0:T(8,128)S(1)}) custom-call(f32[3,8,16,512]{3,2,1,0:T(8,128)} %u_in.1, f32[3,8,16,512]{3,2,1,0:T(8,128)} %f_in.1, f32[8,16,512]{2,1,0:T(8,128)} %st_in.1, f32[8,32]{1,0:T(8,128)} %ap_hbm.1, s32[8,32]{1,0:T(8,128)} %ct_hbm.1, f32[8,32]{1,0:T(8,128)} %p_hbm.1, f32[8,32]{1,0:T(8,128)} %inj_hbm.1), custom_call_target="tpu_custom_call" | custom-call | flops 60000000 | bytes 2700000 | tf_op jit(solution)/shard_map/pallas_call | solution.py:840
  32.1 0.9 %copy.11 = f32[3,8,16,512]{3,2,1,0:T(8,128)} copy(f32[3,8,16,512]{3,2,1,0:T(8,128)S(1)} %get-tuple-element.6) | data formatting | bytes 1572864
  32.9 0.6 %copy.12 = f32[8,32]{1,0:T(8,128)} copy(f32[8,32]{1,0:T(8,128)S(1)} %bitcast.1) | data formatting | bytes 2048
